TPU v7x, 32 devices: a whole 2x2x4 slice. The times are simulated.
32 devices in a mesh: row: 4 (over y, x), col: 8 (over z, core).
Axes of the slice: x: 2, y: 2, z: 4, core: 2. Of those that a mesh axis runs over, the one named last changes fastest.
Arguments:
- object_field: float32 [2, 1536, 2048], P(None, 'row', 'col'), may hold values from -6 to 6
- probe_modes: float32 [2, 2, 128, 128], replicated, may hold values from -2.1 to 2.1
- measured: float32 [4, 8, 8, 128, 128], P('row', 'col'), may hold values from 0.1 to 3
- positions: int32 [4, 8, 2, 8], P('row', 'col'), may hold values from 0 to 383, as said below
- counts: int32 [4, 8], P('row', 'col'), may hold values from 2 to 8, as said below
Outputs:
- object_new: float32 [2, 1536, 2048], P(None, 'row', 'col')
- probe_step: float32 [2, 2, 128, 128], replicated
Inputs may be any that keep to these rules, and one draw needn't show every extreme that they name: `positions`: offsets lie inside the tile: row offsets below 384, column offsets below 256; both edges are reached. `counts`: some tile uses all 8 slots.
All inputs are finite; a program needn't handle non-finite values.
Results may differ from a plain program's by a relative error of at most 0.0003.
Values sent between devices are 32-bit elements; how exact they have to be, the bound alone decides.
A program may use at most 64 MiB of HBM per device.

v0:
```python
import math

import jax
import jax.numpy as jnp
from jax import lax
from jax.sharding import PartitionSpec as P

HIGHEST = lax.Precision.HIGHEST
AMP_FLOOR = 0.25


def shifted(array, axis, by):
    length = lax.axis_size(axis)
    pairs = [(i, i + by) for i in range(length) if 0 <= i + by < length]
    return lax.ppermute(array, axis, pairs)


def fourier_tables(patch_width):
    index = jnp.arange(patch_width, dtype=jnp.int32)
    product = index[:, None] * index[None, :] % patch_width
    angle = product.astype(jnp.float32) * (2.0 * math.pi / patch_width)
    scale = 1.0 / math.sqrt(patch_width)
    return (jnp.cos(angle) * scale, jnp.sin(angle) * scale)


def transform(real_part, imag_part, cosine_table, sine_table, sign_value):
    left_real = jnp.einsum(
        "jk,...kl->...jl", cosine_table, real_part, precision=HIGHEST
    ) - sign_value * jnp.einsum("jk,...kl->...jl", sine_table, imag_part, precision=HIGHEST)
    left_imag = jnp.einsum(
        "jk,...kl->...jl", cosine_table, imag_part, precision=HIGHEST
    ) + sign_value * jnp.einsum("jk,...kl->...jl", sine_table, real_part, precision=HIGHEST)
    out_real = jnp.einsum(
        "...jk,kl->...jl", left_real, cosine_table, precision=HIGHEST
    ) - sign_value * jnp.einsum("...jk,kl->...jl", left_imag, sine_table, precision=HIGHEST)
    out_imag = jnp.einsum(
        "...jk,kl->...jl", left_imag, cosine_table, precision=HIGHEST
    ) + sign_value * jnp.einsum("...jk,kl->...jl", left_real, sine_table, precision=HIGHEST)
    return (out_real, out_imag)


def contributions(patches, probe_modes, amplitudes, live_slots, cosine_table, sine_table):
    patch_real = patches[:, 0][:, None]
    patch_imag = patches[:, 1][:, None]
    mode_real = probe_modes[0][None]
    mode_imag = probe_modes[1][None]
    exit_real = mode_real * patch_real - mode_imag * patch_imag
    exit_imag = mode_real * patch_imag + mode_imag * patch_real
    far_real, far_imag = transform(exit_real, exit_imag, cosine_table, sine_table, -1.0)
    intensity = jnp.sum(far_real * far_real + far_imag * far_imag, axis=1)
    scaling = (amplitudes / jnp.maximum(jnp.sqrt(intensity), AMP_FLOOR) - 1.0) * live_slots[
        :, None, None
    ]
    scaling = scaling[:, None]
    back_real, back_imag = transform(
        far_real * scaling, far_imag * scaling, cosine_table, sine_table, 1.0
    )
    object_real = jnp.sum(mode_real * back_real + mode_imag * back_imag, axis=1)
    object_imag = jnp.sum(mode_real * back_imag - mode_imag * back_real, axis=1)
    probe_real = jnp.sum(patch_real * back_real + patch_imag * back_imag, axis=0)
    probe_imag = jnp.sum(patch_real * back_imag - patch_imag * back_real, axis=0)
    density = jnp.sum(
        live_slots[:, None, None] * (patches[:, 0] * patches[:, 0] + patches[:, 1] * patches[:, 1]),
        axis=0,
    )
    return (
        jnp.stack([object_real, object_imag], axis=1),
        jnp.stack([probe_real, probe_imag]),
        density,
    )


def cut_patches(field, row_starts, col_starts, patch_width):

    def one_patch(row_start, col_start):
        return lax.dynamic_slice(
            field, (jnp.int32(0), row_start, col_start), (2, patch_width, patch_width)
        )

    return jax.vmap(one_patch)(row_starts, col_starts)


def accumulate(gradient, object_terms, row_starts, col_starts):
    patch_width = object_terms.shape[-1]

    def add_one(slot_index, totals):
        corner_at = (jnp.int32(0), row_starts[slot_index], col_starts[slot_index])
        current = lax.dynamic_slice(totals, corner_at, (2, patch_width, patch_width))
        return lax.dynamic_update_slice(totals, current + object_terms[slot_index], corner_at)

    return lax.fori_loop(0, object_terms.shape[0], add_one, gradient)


def per_device(object_field, probe_modes, measured, positions, counts):
    patch_width = probe_modes.shape[-1]
    tile_height, tile_width = (object_field.shape[1], object_field.shape[2])
    cosine_table, sine_table = fourier_tables(patch_width)
    row_starts = positions[0, 0, 0]
    col_starts = positions[0, 0, 1]
    capacity = row_starts.shape[0]
    live_slots = (jnp.arange(capacity, dtype=jnp.int32) < counts[0, 0]).astype(jnp.float32)
    amplitudes = measured[0, 0]
    from_below = shifted(object_field[:, :patch_width, :], "row", -1)
    taller = jnp.concatenate([object_field, from_below], axis=1)
    from_right = shifted(taller[:, :, :patch_width], "col", -1)
    extended = jnp.concatenate([taller, from_right], axis=2)
    patches = cut_patches(extended, row_starts, col_starts, patch_width)
    object_terms, probe_terms, density = contributions(
        patches, probe_modes, amplitudes, live_slots, cosine_table, sine_table
    )
    gradient = accumulate(jnp.zeros_like(extended), object_terms, row_starts, col_starts)
    spilled = shifted(gradient[:, :, tile_width:], "col", 1)
    narrow = gradient[:, :, :tile_width].at[:, :, :patch_width].add(spilled)
    lower_rim = shifted(narrow[:, tile_height:, :], "row", 1)
    own_part = narrow[:, :tile_height, :].at[:, :patch_width, :].add(lower_rim)
    peak_power = jnp.max(jnp.sum(probe_modes * probe_modes, axis=(0, 1)))
    object_new = object_field + own_part / (peak_power + 1e-06)
    probe_sum, density_sum = lax.psum((probe_terms, density), ("row", "col"))
    probe_step = probe_sum / jnp.sqrt(density_sum + 1.0)[None, None]
    return (object_new, probe_step)


def solution(mesh):
    in_specs = (
        P(None, "row", "col"),
        P(),
        P("row", "col", None, None, None),
        P("row", "col", None, None),
        P("row", "col"),
    )
    out_specs = (P(None, "row", "col"), P())
    return jax.shard_map(
        per_device, mesh=mesh, in_specs=in_specs, out_specs=out_specs, check_vma=False
    )
```

profile of v0, /device:TPU:0, one launch (start us, length us, event | category | flops | bytes accessed | tf_op | source)
XLA Modules:
  0.0 282.9 jit_solution(5196106490224885881)
XLA Ops:
  7.2 1.0 slice.93
  8.2 1.3 collective-permute-start
  11.0 1.2 constant_dynamic-update-slice_fusion.1
  12.2 7.1 %collective-permute-done = f32[2,128,256]{2,1,0:T(8,128)S(1)} collective-permute-done((f32[2,128,256]{2,1,0:T(8,128)S(1)}, f32[2,128,256]{2,1,0:T(8,128)S(1)}, u32[]{:S(2)}, u32[]{:S(2)}) %collective-permute-start) | collective-permute-done | bytes 262176 | tf_op jit(solution)/shard_map/ppermute | solution.py:15
  19.4 1.3 collective-permute-start.1
  20.8 2.4 collective-permute-done.1
  23.3 16.4 %while.17 = (s32[]{:T(128)}, f32[2,512,384]{2,1,0:T(8,128)S(1)}, s32[8,3]{0,1:T(4,128)S(1)}, f32[8,2,128,128]{3,2,1,0:T(8,128)S(1)}, s32[]{:T(128)}) while((s32[]{:T(128)}, f32[2,512,384]{2,1,0:T(8,128)S(1)}, s32[8,3]{0,1:T(4,128)S(1)}, f32[8,2,128,128]{3,2,1,0:T(8,128)S(1)}, s32[]{:T(128)}) %tuple.63), condition=%wide.while_cond.2, body=%wide.while_body.2.sunk | while | flops 2 | bytes 262261 | solution.py:76
  24.0 1.4 bitcast_dynamic-update-slice_fusion.2
  26.0 1.4 bitcast_dynamic-update-slice_fusion.2
  28.1 1.4 bitcast_dynamic-update-slice_fusion.2
  30.1 1.4 bitcast_dynamic-update-slice_fusion.2
  32.2 1.4 bitcast_dynamic-update-slice_fusion.2
  34.2 1.4 bitcast_dynamic-update-slice_fusion.2
  36.3 1.4 bitcast_dynamic-update-slice_fusion.2
  38.3 1.4 bitcast_dynamic-update-slice_fusion.2
  39.8 2.0 fusion.8
  41.8 2.0 fusion.9
  43.8 2.0 fusion.5
  45.9 2.1 fusion.7
  47.9 1.9 fusion.59
  49.9 2.1 fusion.56
  52.0 2.0 fusion.3
  54.0 2.0 add_reduce_fusion.2
  56.0 0.9 multiply_reduce_fusion
  56.9 2.0 fusion.14
  58.9 2.0 fusion.10
  60.9 2.0 fusion
  62.9 2.2 fusion.1
  65.1 2.0 fusion.53
  67.1 1.9 fusion.50
  69.0 2.0 convolution_subtract_fusion
  71.0 2.5 add_reduce_fusion
  73.7 60.3 %while.16 = (s32[]{:T(128)}, f32[2,512,384]{2,1,0:T(8,128)S(1)}, s32[8]{0:T(128)S(1)}, s32[8]{0:T(128)S(1)}, f32[8,2,128,128]{3,2,1,0:T(8,128)S(1)}, /*index=5*/s32[]{:T(128)}, s32[]{:T(128)}, s32[]{:T(128)}, s32[]{:T(128)}) while((s32[]{:T(128)}, f32[2,512,384]{2,1,0:T(8,128)S(1)}, s32[8]{0:T(128)S(1)}, s32[8]{0:T(128)S(1)}, ...), condition=%wide.region_4.5_spmd, body=%wide.region_3.4_spmd.sunk | while | flops 32776 | bytes 655561 | solution.py:91
  78.9 2.1 dynamic_update_slice.8
  86.2 1.7 dynamic_update_slice.8
  93.1 2.3 dynamic_update_slice.8
  100.6 2.5 dynamic_update_slice.8
  108.3 2.5 dynamic_update_slice.8
  116.0 2.5 dynamic_update_slice.8
  123.8 2.5 dynamic_update_slice.8
  131.5 2.5 dynamic_update_slice.8
  134.8 10.6 %collective-permute-start.2 = (f32[2,512,128]{2,1,0:T(8,128)}, f32[2,512,128]{2,1,0:T(8,128)}, u32[]{:S(2)}, u32[]{:S(2)}) collective-permute-start(f32[2,512,128]{2,1,0:T(8,128)} %slice.100), channel_id=1, source_target_pairs={{0,1},{1,2},{2,3},{3,4},{4,5},{5,6},{6,7},{8,9},{9,10},{10,11},{11... | collective-permute-start | bytes 1572872 | tf_op jit(solution)/shard_map/ppermute | solution.py:15
  147.5 1.1 add_dynamic-update-slice_fusion
  148.6 4.2 %collective-permute-start.3 = (f32[2,128,256]{2,1,0:T(8,128)S(1)}, f32[2,128,256]{2,1,0:T(8,128)S(1)}, u32[]{:S(2)}, u32[]{:S(2)}) collective-permute-start(f32[2,128,256]{2,1,0:T(8,128)S(1)} %slice.123), channel_id=1, source_target_pairs={{0,8},{8,16},{16,24},{1,9},{9,17},{17,25},{2,10},{10,18},{18,26},{... | collective-permute-start | bytes 786440 | tf_op jit(solution)/shard_map/ppermute | solution.py:15
  152.8 119.6 %all-reduce.3.cloned.1.call-done = (f32[2,2,128,128]{3,2,1,0:T(8,128)}, f32[128,128]{1,0:T(8,128)}) async-done(((f32[2,2,128,128]{3,2,1,0:T(8,128)}, f32[128,128]{1,0:T(8,128)}), (f32[2,2,128,128]{3,2,1,0:T(8,128)}, f32[128,128]{1,0:T(8,128)})) %all-reduce.3.cloned.1.call-update) | async-done | bytes 327696 | tf_op jit(solution)/shard_map/psum | solution.py:118
  272.5 0.9 add_sqrt_fusion
  273.3 1.7 broadcast_divide_fusion
  275.1 1.0 divide_add_fusion
  (74 shorter events, 19.4 us)
Async XLA Ops:
  7.2 265.3 %all-reduce.3.cloned.1.call-start = ((), (), s32[]{:S(2)}) async-start(), calls=%async_computation | async-start | bytes 655360 | tf_op jit(solution)/shard_map/psum | solution.py:118
  8.2 11.1 %collective-permute-start = (f32[2,128,256]{2,1,0:T(8,128)S(1)}, f32[2,128,256]{2,1,0:T(8,128)S(1)}, u32[]{:S(2)}, u32[]{:S(2)}) collective-permute-start(f32[2,128,256]{2,1,0:T(8,128)S(1)} %slice.93), channel_id=1, source_target_pairs={{8,0},{16,8},{24,16},{9,1},{17,9},{25,17},{10,2},{18,10},{26,18},{... | collective-permute-start | bytes 786440 | tf_op jit(solution)/shard_map/ppermute | solution.py:15
  10.9 9.8 %copy-start.3 = (s32[1,1,2,8]{3,2,1,0:T(2,128)S(1)}, s32[1,1,2,8]{3,2,1,0:T(2,128)}, u32[]{:S(2)}) copy-start(s32[1,1,2,8]{3,2,1,0:T(2,128)} %param.14) | copy-start | bytes 196
  10.9 9.8 %copy-start.1 = (f32[2,2,128,128]{3,2,1,0:T(8,128)S(1)}, f32[2,2,128,128]{3,2,1,0:T(8,128)}, u32[]{:S(2)}) copy-start(f32[2,2,128,128]{3,2,1,0:T(8,128)} %param.12) | copy-start | bytes 786436
  19.4 3.8 %collective-permute-start.1 = (f32[2,512,128]{2,1,0:T(8,128)S(1)}, f32[2,512,128]{2,1,0:T(8,128)S(1)}, u32[]{:S(2)}, u32[]{:S(2)}) collective-permute-start(f32[2,512,128]{2,1,0:T(8,128)S(1)} %slice.119), channel_id=1, source_target_pairs={{1,0},{2,1},{3,2},{4,3},{5,4},{6,5},{7,6},{9,8},{10,9},{11,10},{12... | collective-permute-start | bytes 1572872 | tf_op jit(solution)/shard_map/ppermute | solution.py:15
  54.0 2.0 copy-start.2
  134.8 12.7 %collective-permute-start.2 = (f32[2,512,128]{2,1,0:T(8,128)}, f32[2,512,128]{2,1,0:T(8,128)}, u32[]{:S(2)}, u32[]{:S(2)}) collective-permute-start(f32[2,512,128]{2,1,0:T(8,128)} %slice.100), channel_id=1, source_target_pairs={{0,1},{1,2},{2,3},{3,4},{4,5},{5,6},{6,7},{8,9},{9,10},{10,11},{11... | collective-permute-start | bytes 1572872 | tf_op jit(solution)/shard_map/ppermute | solution.py:15
  148.6 126.5 %copy-start = (f32[2,384,256]{2,1,0:T(8,128)S(1)}, f32[2,384,256]{2,1,0:T(8,128)}, u32[]{:S(2)}) copy-start(f32[2,384,256]{2,1,0:T(8,128)} %param.11) | copy-start | bytes 2359300
  148.6 126.4 %collective-permute-start.3 = (f32[2,128,256]{2,1,0:T(8,128)S(1)}, f32[2,128,256]{2,1,0:T(8,128)S(1)}, u32[]{:S(2)}, u32[]{:S(2)}) collective-permute-start(f32[2,128,256]{2,1,0:T(8,128)S(1)} %slice.123), channel_id=1, source_target_pairs={{0,8},{8,16},{16,24},{1,9},{9,17},{17,25},{2,10},{10,18},{18,26},{... | collective-permute-start | bytes 786440 | tf_op jit(solution)/shard_map/ppermute | solution.py:15
Sparse Core Ops, SparseCore 0:
  147.6 124.7 all-reduce.2
where the time goes:
time: 284 us; the launch traced here: 283 us
  waiting for transfers between devices  129 us (45%)
  local copies, waits for them, and re-layouts  47.7 us (17%)
  matrix products  32.6 us (11%)
  loops' own time  31.5 us (11%)
  starting transfers between devices  17.4 us (6%)
  between operations  15.7 us (6%)
  other arithmetic  8.78 us (3%)
    psum x1, waiting for transfers between devices, per_device(): probe_sum, density_sum = lax.psum((probe_terms, density), ('row', 'col'))  120 us
    another operation x1, loops' own time, accumulate(): return lax.fori_loop(0, object_terms.shape[0], add_one, gradient)  31.4 us
    dynamic_update_slice x8, local copies, waits for them, and re-layouts, add_one(): lax.dynamic_update_slice(totals, current + object_terms[slot_index], corn...  18.6 us
    ppermute x4, starting transfers between devices, shifted(): return lax.ppermute(array, axis, pairs)  17.3 us
    gather x24, local copies, waits for them, and re-layouts  16.2 us
    ppermute x4, waiting for transfers between devices, shifted(): return lax.ppermute(array, axis, pairs)  9.58 us
    dynamic_slice x16, local copies, waits for them, and re-layouts, add_one(): corner_at = (jnp.int32(0), row_starts[slot_index], col_starts[slot_index])  9.42 us
  transfers between devices with their start and end apart: 5, of which 3 were waited for; matrix products, arithmetic and copies ran while one was open for 3% of the time, Pallas kernels for 0%

commit v1 on v0

v1 whole, which is shorter than its diff:
```python
import functools
import math

import jax
import jax.numpy as jnp
import ml_dtypes
import numpy as np
from jax import lax
from jax.experimental import pallas as pl
from jax.experimental.pallas import tpu as pltpu
from jax.sharding import PartitionSpec as P

AMP_FLOOR = 0.25
F32 = jnp.float32
MESH = pl.DeviceIdType.MESH
VMEM = pl.BlockSpec(memory_space=pltpu.VMEM)
SMEM = pl.BlockSpec(memory_space=pltpu.SMEM)
LIMIT = 48 * 1024 * 1024


def fourier_tables(n):
    index = np.arange(n)
    angle = (index[:, None] * index[None, :] % n) * (2.0 * math.pi / n)
    c = np.cos(angle) / math.sqrt(n)
    s = np.sin(angle) / math.sqrt(n)
    a = np.block([[c, -s], [s, c]]).astype(np.float32)
    parts = []
    for w in (a, a.T):
        hi = w.astype(ml_dtypes.bfloat16)
        lo = (w - hi.astype(np.float32)).astype(ml_dtypes.bfloat16)
        parts += [hi, lo]
    return np.stack(parts)


def split(x):
    hi = x.astype(jnp.bfloat16)
    return hi, (x - hi.astype(F32)).astype(jnp.bfloat16)


def dot(a, b):
    return jnp.dot(a, b, preferred_element_type=F32)


def left(w_hi, w_lo, x):
    hi, lo = split(x)
    return dot(w_hi, hi) + (dot(w_hi, lo) + dot(w_lo, hi))


def right(x, w_hi, w_lo):
    hi, lo = split(x)
    return dot(hi, w_hi) + (dot(lo, w_hi) + dot(hi, w_lo))


def swap_blocks(x, n):
    return jnp.concatenate(
        [
            jnp.concatenate([x[:n, :n], x[n:, :n]], axis=1),
            jnp.concatenate([x[:n, n:], x[n:, n:]], axis=1),
        ],
        axis=0,
    )


def tiling(nrow, ncol, n):
    tiles = 5 * (n // 8)
    share = -(-tiles // nrow)
    part = -(-share // ncol)
    return tiles, share, part


def place():
    return lax.axis_index("row"), lax.axis_index("col")


def halo_kernel(nrow, ncol, n, obj_ref, ext_ref, send_sem, recv_sem):
    _, height, width = obj_ref.shape
    r, c = place()
    up, down = lax.rem(r + nrow - 1, nrow), lax.rem(r + 1, nrow)
    west, east = lax.rem(c + ncol - 1, ncol), lax.rem(c + 1, ncol)
    barrier = pltpu.get_barrier_semaphore()
    for peer in ((up, c), (down, c), (r, west), (r, east), (up, west), (down, east)):
        pl.semaphore_signal(barrier, inc=1, device_id=peer, device_id_type=MESH)
    pl.semaphore_wait(barrier, 6)

    def copy(index, src, dst, peer):
        return pltpu.make_async_remote_copy(
            src_ref=src,
            dst_ref=dst,
            send_sem=send_sem.at[index],
            recv_sem=recv_sem.at[index],
            device_id=peer,
            device_id_type=MESH,
        )

    blocks = width // n
    right_halo = ext_ref.at[:, blocks, :height]
    corner_halo = ext_ref.at[:, blocks, height:]
    copies = [
        (copy(0, obj_ref.at[:, :, :n], right_halo, (r, west)), c > 0, c < ncol - 1, right_halo),
        (
            copy(1, obj_ref.at[:, :n, :n], corner_halo, (up, west)),
            (r > 0) & (c > 0),
            (r < nrow - 1) & (c < ncol - 1),
            corner_halo,
        ),
    ]
    for b in range(blocks):
        halo = ext_ref.at[:, b, height:]
        source = obj_ref.at[:, :n, b * n : (b + 1) * n]
        copies.append((copy(2 + b, source, halo, (up, c)), r > 0, r < nrow - 1, halo))
    for one, sends, _, _ in copies:

        @pl.when(sends)
        def _():
            one.start()

    for b in range(blocks):
        ext_ref[:, b, :height] = obj_ref[:, :, b * n : (b + 1) * n]
    for one, sends, takes, halo in copies:

        @pl.when(jnp.logical_not(takes))
        def _():
            halo[...] = jnp.zeros(halo.shape, F32)

        @pl.when(takes)
        def _():
            one.wait_recv()

        @pl.when(sends)
        def _():
            one.wait_send()


def compute_kernel(
    shares, height, width, pos_ref, cnt_ref, ext_ref, probe_ref, meas_ref, table_ref, grad_ref, red_ref, sums
):
    n = probe_ref.shape[-1]
    slots = meas_ref.shape[0]
    tiles, share, padded = shares
    a_hi, a_lo, b_hi, b_lo = (table_ref[i] for i in range(4))
    pr = [probe_ref[0, 0], probe_ref[0, 1]]
    pi = [probe_ref[1, 0], probe_ref[1, 1]]
    power = pr[0] * pr[0] + pi[0] * pi[0] + (pr[1] * pr[1] + pi[1] * pi[1])
    inverse = 1.0 / (jnp.max(power, keepdims=True) + 1e-06)
    lane = lax.broadcasted_iota(jnp.int32, (n, n), 1)
    blocks = width // n
    grad_ref[...] = jnp.zeros(grad_ref.shape, F32)
    grad_ref[:, :blocks, :height] = ext_ref[:, :blocks, :height]
    sums[...] = jnp.zeros(sums.shape, F32)

    def one_slot(s, carry):
        row, col = pos_ref[0, s], pos_ref[1, s]
        live = jnp.where(s < cnt_ref[0, 0], 1.0, 0.0).astype(F32)
        near = col // n
        shift = lax.rem(col, n)
        back_shift = lax.rem(n - shift, n)
        rows = pl.ds(row, n)

        def cut(part):
            a = pltpu.roll(ext_ref[part, near, rows], back_shift, 1)
            b = pltpu.roll(ext_ref[part, near + 1, rows], back_shift, 1)
            return jnp.where(lane < n - shift, a, b)

        qr, qi = cut(0), cut(1)
        waves = jnp.concatenate(
            [
                jnp.concatenate([pr[m] * qr - pi[m] * qi for m in range(2)], axis=1),
                jnp.concatenate([pr[m] * qi + pi[m] * qr for m in range(2)], axis=1),
            ],
            axis=0,
        )
        far = right(swap_blocks(left(b_hi, b_lo, waves), n), a_hi, a_lo)
        squares = far * far
        intensity = squares[:n, :n] + squares[:n, n:] + (squares[n:, :n] + squares[n:, n:])
        scaling = (meas_ref[s] * lax.rsqrt(jnp.maximum(intensity, AMP_FLOOR * AMP_FLOOR)) - 1.0) * live
        scaling = jnp.concatenate([scaling, scaling], axis=1)
        scaling = jnp.concatenate([scaling, scaling], axis=0)
        back = left(a_hi, a_lo, swap_blocks(right(far * scaling, b_hi, b_lo), n))
        br = [back[:n, :n], back[:n, n:]]
        bi = [back[n:, :n], back[n:, n:]]
        for m in range(2):
            sums[m] += qr * br[m] + qi * bi[m]
            sums[2 + m] += qr * bi[m] - qi * br[m]
        sums[4] += live * (qr * qr + qi * qi)
        terms = (
            pr[0] * br[0] + pi[0] * bi[0] + (pr[1] * br[1] + pi[1] * bi[1]),
            pr[0] * bi[0] - pi[0] * br[0] + (pr[1] * bi[1] - pi[1] * br[1]),
        )
        for part in range(2):
            term = pltpu.roll(terms[part] * inverse, shift, 1)
            grad_ref[part, near, rows] += jnp.where(lane >= shift, term, 0.0)
            grad_ref[part, near + 1, rows] += jnp.where(lane < shift, term, 0.0)
        return carry

    lax.fori_loop(0, slots, one_slot, 0)
    per = n // 8
    if padded > share or share * red_ref.shape[0] > tiles:
        red_ref[...] = jnp.zeros(red_ref.shape, F32)
    for g in range(tiles):
        red_ref[g // share, g % share] = sums[g // per, 8 * (g % per) : 8 * (g % per) + 8]


def finish_kernel(
    nrow, ncol, n, shares,
    grad_ref, red_ref, obj_ref, probe_ref,
    got1, acc1, got2, acc2, all2, all1, in_right, in_below, in_corner,
    send1, recv1, send2, recv2, send3, recv3, send4, recv4, send_halo, recv_halo,
):
    _, height, width = obj_ref.shape
    tiles, share, part = shares
    blocks = width // n
    r, c = place()
    up, down = lax.rem(r + nrow - 1, nrow), lax.rem(r + 1, nrow)
    west, east = lax.rem(c + ncol - 1, ncol), lax.rem(c + 1, ncol)
    row_peer = lambda d: (lax.rem(r + d, nrow), c)
    col_peer = lambda d: (r, lax.rem(c + d, ncol))
    barrier = pltpu.get_barrier_semaphore()
    peers = [row_peer(d) for d in range(1, nrow)] + [col_peer(d) for d in range(1, ncol)]
    for peer in peers + [(up, west), (down, east)]:
        pl.semaphore_signal(barrier, inc=1, device_id=peer, device_id_type=MESH)
    pl.semaphore_wait(barrier, nrow + ncol)

    def copy(src, dst, send_sem, recv_sem, peer):
        return pltpu.make_async_remote_copy(
            src_ref=src,
            dst_ref=dst,
            send_sem=send_sem,
            recv_sem=recv_sem,
            device_id=peer,
            device_id_type=MESH,
        )

    first = []
    for d in range(1, nrow):
        peer = row_peer(d)
        first.append(copy(red_ref.at[peer[0]], got1.at[r], send1.at[d], recv1.at[d], peer))
        first[-1].start()

    spills = (
        (copy(grad_ref.at[:, blocks, :height], in_right, send_halo.at[0], recv_halo.at[0], (r, east)), c < ncol - 1, c > 0),
        (copy(grad_ref.at[:, :blocks, height:], in_below, send_halo.at[1], recv_halo.at[1], (down, c)), r < nrow - 1, r > 0),
        (
            copy(grad_ref.at[:, blocks, height:], in_corner, send_halo.at[2], recv_halo.at[2], (down, east)),
            (r < nrow - 1) & (c < ncol - 1),
            (r > 0) & (c > 0),
        ),
    )
    for one, sends, _ in spills:

        @pl.when(sends)
        def _():
            one.start()

    for b in range(blocks):
        obj_ref[:, :, b * n : (b + 1) * n] = grad_ref[:, b, :height]

    for one in first:
        one.wait_recv()
    total = red_ref[r]
    for d in range(1, nrow):
        total = total + got1[lax.rem(r + nrow - d, nrow)]
    acc1[...] = total.reshape(acc1.shape)

    second = []
    for d in range(1, ncol):
        peer = col_peer(d)
        second.append(copy(acc1.at[peer[1]], got2.at[c], send2.at[d], recv2.at[d], peer))
        second[-1].start()
    for one in second:
        one.wait_recv()
    total = acc1[c]
    for d in range(1, ncol):
        total = total + got2[lax.rem(c + ncol - d, ncol)]
    acc2[...] = total

    third = []
    for d in range(1, ncol):
        third.append(copy(acc2, all2.at[c], send3.at[d], recv3.at[d], col_peer(d)))
        third[-1].start()
    all2[c] = total

    for (one, _, takes), got in zip(spills, (in_right, in_below, in_corner)):

        @pl.when(takes)
        def _():
            one.wait_recv()
            if got is in_right:
                obj_ref[:, :, :n] += got[...]
            elif got is in_corner:
                obj_ref[:, :n, :n] += got[...]
            else:
                for b in range(blocks):
                    obj_ref[:, :n, b * n : (b + 1) * n] += got[:, b]

    for one in third:
        one.wait_recv()

    fourth = []
    for d in range(1, nrow):
        fourth.append(copy(all2, all1.at[r], send4.at[d], recv4.at[d], row_peer(d)))
        fourth[-1].start()
    all1[r] = all2[...]
    for one in fourth:
        one.wait_recv()

    per = n // 8

    def tile(g):
        k = g % share
        return all1[g // share, k // part, k % part]

    for i in range(per):
        factor = lax.rsqrt(tile(4 * per + i) + 1.0)
        for ch in range(4):
            probe_ref[ch // 2, ch % 2, 8 * i : 8 * i + 8] = tile(ch * per + i) * factor

    for one in first + second + third + fourth:
        one.wait_send()
    for one, sends, _ in spills:

        @pl.when(sends)
        def _():
            one.wait_send()


def per_device(nrow, ncol, table, object_field, probe_modes, measured, positions, counts):
    n = probe_modes.shape[-1]
    _, height, width = object_field.shape
    tiles, share, part = tiling(nrow, ncol, n)
    params = functools.partial(pltpu.CompilerParams, vmem_limit_bytes=LIMIT)
    extended = pl.pallas_call(
        functools.partial(halo_kernel, nrow, ncol, n),
        out_shape=jax.ShapeDtypeStruct((2, width // n + 1, height + n, n), F32),
        in_specs=[VMEM],
        out_specs=VMEM,
        scratch_shapes=[pltpu.SemaphoreType.DMA((2 + width // n,))] * 2,
        compiler_params=params(collective_id=0, has_side_effects=True),
    )(object_field)
    gradient, sums = pl.pallas_call(
        functools.partial(compute_kernel, (tiles, share, ncol * part), height, width),
        out_shape=(
            jax.ShapeDtypeStruct((2, width // n + 1, height + n, n), F32),
            jax.ShapeDtypeStruct((nrow, ncol * part, 8, n), F32),
        ),
        in_specs=[SMEM, SMEM, VMEM, VMEM, VMEM, VMEM],
        out_specs=(VMEM, VMEM),
        scratch_shapes=[pltpu.VMEM((5, n, n), F32)],
        compiler_params=params(),
    )(positions[0, 0], counts, extended, probe_modes, measured[0, 0], table)
    dma = pltpu.SemaphoreType.DMA
    return pl.pallas_call(
        functools.partial(finish_kernel, nrow, ncol, n, (tiles, share, part)),
        out_shape=(
            jax.ShapeDtypeStruct((2, height, width), F32),
            jax.ShapeDtypeStruct((2, 2, n, n), F32),
        ),
        in_specs=[VMEM, VMEM],
        out_specs=(VMEM, VMEM),
        scratch_shapes=[
            pltpu.VMEM((nrow, ncol * part, 8, n), F32),
            pltpu.VMEM((ncol, part, 8, n), F32),
            pltpu.VMEM((ncol, part, 8, n), F32),
            pltpu.VMEM((part, 8, n), F32),
            pltpu.VMEM((ncol, part, 8, n), F32),
            pltpu.VMEM((nrow, ncol, part, 8, n), F32),
            pltpu.VMEM((2, height, n), F32),
            pltpu.VMEM((2, width // n, n, n), F32),
            pltpu.VMEM((2, n, n), F32),
        ]
        + [dma((k,)) for k in (nrow, nrow, ncol, ncol, ncol, ncol, nrow, nrow, 3, 3)],
        compiler_params=params(collective_id=1, has_side_effects=True),
    )(gradient, sums)


def solution(mesh):
    nrow, ncol = mesh.shape["row"], mesh.shape["col"]
    in_specs = (
        P(None, "row", "col"),
        P(),
        P("row", "col", None, None, None),
        P("row", "col", None, None),
        P("row", "col"),
    )
    out_specs = (P(None, "row", "col"), P())

    def run(object_field, probe_modes, measured, positions, counts):
        table = jnp.asarray(fourier_tables(probe_modes.shape[-1]))
        return jax.shard_map(
            functools.partial(per_device, nrow, ncol, table),
            mesh=mesh, in_specs=in_specs, out_specs=out_specs, check_vma=False,
        )(object_field, probe_modes, measured, positions, counts)

    return run
```

time: 284 us -> 56.8 us (0.20)
  waiting for transfers between devices: 129 us -> 0 us
  Pallas kernels: 0 us -> 52.6 us
  local copies, waits for them, and re-layouts: 47.7 us -> 2.73 us
  matrix products: 32.6 us -> 0 us
  loops' own time: 31.5 us -> 0 us
  starting transfers between devices: 17.4 us -> 0 us
  between operations: 15.7 us -> 1.36 us
  other arithmetic: 8.78 us -> 0 us
    psum x1 -> x0, waiting for transfers between devices: 120 us -> none  [per_device(): probe_sum, density_sum = lax.psum((probe_terms, density), ('row', 'col'))]
    pallas_call x0 -> x3, Pallas kernels: none -> 52.6 us  [the longest x1 25.1 us: per_device(): pl.pallas_call(functools.partial(finish_kernel, nrow, ncol, n, (tiles, sh...]
    dot_general x16 -> x0, matrix products: 32.6 us -> none  [the longest x2 4.47 us: transform(): jnp.einsum('...jk,kl->...jl', left_real, sine_table, precision=HIGHEST)]
    another operation x2 -> x0, loops' own time: 31.5 us -> none  [the longest x1 31.4 us: accumulate(): return lax.fori_loop(0, object_terms.shape[0], add_one, gradient)]
    dynamic_update_slice x8 -> x0, local copies, waits for them, and re-layouts: 18.6 us -> none  [add_one(): lax.dynamic_update_slice(totals, current + object_terms[slot_index], corn...]
    ppermute x4 -> x0, starting transfers between devices: 17.3 us -> none  [shifted(): return lax.ppermute(array, axis, pairs)]
    gather x24 -> x0, local copies, waits for them, and re-layouts: 16.2 us -> none
    ppermute x4 -> x0, waiting for transfers between devices: 9.58 us -> none  [shifted(): return lax.ppermute(array, axis, pairs)]
  transfers between devices with their start and end apart: 5 -> 0, of which waited for: 3 -> 0; matrix products, arithmetic and copies ran while one was open for 3% -> 0% of each run, Pallas kernels for 0% -> 0%
where the time goes in v1:
time: 56.8 us; the launch traced here: 56.7 us
  Pallas kernels  52.6 us (93%)
  local copies, waits for them, and re-layouts  2.73 us (5%)
  between operations  1.36 us (2%)
    pallas_call x1, Pallas kernels, per_device(): pl.pallas_call(functools.partial(finish_kernel, nrow, ncol, n, (tiles, sh...  25.1 us
    pallas_call x1, Pallas kernels, per_device(): pl.pallas_call(functools.partial(halo_kernel, nrow, ncol, n), out_shape=j...  14.6 us
    pallas_call x1, Pallas kernels, per_device(): pl.pallas_call(functools.partial(compute_kernel, (tiles, share, ncol * pa...  12.8 us
    unnamed x12, local copies, waits for them, and re-layouts  2.73 us

profile of v1, /device:TPU:0, one launch (start us, length us, event | category | flops | bytes accessed | tf_op | source)
XLA Modules:
  0.0 56.7 jit_solution(72307671735562745)
XLA Ops:
  0.6 0.0 copy-start.4
  1.3 0.0 copy-start
  1.3 1.1 %copy-done = f32[2,384,256]{2,1,0:T(8,128)S(1)} copy-done((f32[2,384,256]{2,1,0:T(8,128)S(1)}, f32[2,384,256]{2,1,0:T(8,128)}, u32[]{:S(2)}) %copy-start) | copy-done | bytes 786456
  2.4 0.0 copy-start.1
  2.4 0.0 copy-start.2
  2.4 0.0 copy-start.3
  2.4 14.6 %shard_map.77.ext_ref = f32[2,3,512,128]{3,2,1,0:T(8,128)S(1)} custom-call(f32[2,384,256]{2,1,0:T(8,128)S(1)} %copy-done), custom_call_target="tpu_custom_call" | custom-call | tf_op jit(solution)/shard_map/pallas_call | solution.py:331
  17.1 0.0 copy-done.4
  17.1 0.0 copy-done.1
  17.1 0.0 copy-done.2
  17.1 0.0 copy-done.3
  17.1 12.8 %shard_map.78 = (f32[2,3,512,128]{3,2,1,0:T(8,128)S(1)}, f32[4,24,8,128]{3,2,1,0:T(8,128)S(1)}) custom-call(s32[2,8]{1,0:T(2,128)S(1)} %bitcast.3, s32[1,1]{1,0:T(1,128)S(6)} %copy.10.cnt_ref, f32[2,3,512,128]{3,2,1,0:T(8,128)S(1)} %shard_map.77.ext_ref, f32[2,2,128,128]{3,2,1,0:T(8,128)S(1)} %copy-done.3, f32[8,128,128]{2,1,0:T(8,128)S(1)} %bitcast.2, ...), custom_call_target="tpu_custom_call" | custom-call | tf_op jit(solution)/shard_map/pallas_call | solution.py:339
  30.0 25.1 %shard_map.79 = (f32[2,384,256]{2,1,0:T(8,128)S(1)}, f32[2,2,128,128]{3,2,1,0:T(8,128)S(1)}) custom-call(f32[2,3,512,128]{3,2,1,0:T(8,128)S(1)} %get-tuple-element.4.grad_ref, f32[4,24,8,128]{3,2,1,0:T(8,128)S(1)} %get-tuple-element.5.red_ref), custom_call_target="tpu_custom_call" | custom-call | tf_op jit(solution)/shard_map/pallas_call | solution.py:351
  55.1 0.9 %copy.11 = f32[2,384,256]{2,1,0:T(8,128)} copy(f32[2,384,256]{2,1,0:T(8,128)S(1)} %get-tuple-element.8) | data formatting | bytes 1572864
  56.0 0.7 %copy.12 = f32[2,2,128,128]{3,2,1,0:T(8,128)} copy(f32[2,2,128,128]{3,2,1,0:T(8,128)S(1)} %get-tuple-element.9) | data formatting | bytes 524288
Async XLA Ops:
  0.6 16.4 %copy-start.4 = (s32[1,1,2,8]{3,2,1,0:T(2,128)S(1)}, s32[1,1,2,8]{3,2,1,0:T(2,128)}, u32[]{:S(2)}) copy-start(s32[1,1,2,8]{3,2,1,0:T(2,128)} %param.9) | copy-start | bytes 196
  1.3 1.1 %copy-start = (f32[2,384,256]{2,1,0:T(8,128)S(1)}, f32[2,384,256]{2,1,0:T(8,128)}, u32[]{:S(2)}) copy-start(f32[2,384,256]{2,1,0:T(8,128)} %obj_ref.1) | copy-start | bytes 2359300
  2.4 14.6 %copy-start.1 = (f32[1,1,8,128,128]{4,3,2,1,0:T(8,128)S(1)}, f32[1,1,8,128,128]{4,3,2,1,0:T(8,128)}, u32[]{:S(2)}) copy-start(f32[1,1,8,128,128]{4,3,2,1,0:T(8,128)} %param.8) | copy-start | bytes 1572868
  2.4 14.7 %copy-start.2 = (bf16[4,256,256]{2,1,0:T(8,128)(2,1)S(1)}, bf16[4,256,256]{2,1,0:T(8,128)(2,1)}, u32[]{:S(2)}) copy-start(bf16[4,256,256]{2,1,0:T(8,128)(2,1)} %constant.2.clone.table_ref) | copy-start | bytes 1572868
  2.4 14.7 %copy-start.3 = (f32[2,2,128,128]{3,2,1,0:T(8,128)S(1)}, f32[2,2,128,128]{3,2,1,0:T(8,128)}, u32[]{:S(2)}) copy-start(f32[2,2,128,128]{3,2,1,0:T(8,128)} %probe_ref.1) | copy-start | bytes 786436

commit v2 on v1

v2 whole, which is shorter than its diff:
```python
import functools
import math

import jax
import jax.numpy as jnp
import ml_dtypes
import numpy as np
from jax import lax
from jax.experimental import pallas as pl
from jax.experimental.pallas import tpu as pltpu
from jax.sharding import PartitionSpec as P

AMP_FLOOR = 0.25
F32 = jnp.float32
MESH = pl.DeviceIdType.MESH
VMEM = pl.BlockSpec(memory_space=pltpu.VMEM)
SMEM = pl.BlockSpec(memory_space=pltpu.SMEM)
LIMIT = 48 * 1024 * 1024


def fourier_tables(n):
    index = np.arange(n)
    angle = (index[:, None] * index[None, :] % n) * (2.0 * math.pi / n)
    c = np.cos(angle) / math.sqrt(n)
    s = np.sin(angle) / math.sqrt(n)
    a = np.block([[c, -s], [s, c]]).astype(np.float32)
    on_left, on_right = [], []
    for w in (a, a.T):
        hi = w.astype(ml_dtypes.bfloat16)
        lo = (w - hi.astype(np.float32)).astype(ml_dtypes.bfloat16)
        on_left.append(np.concatenate([hi, lo, hi], axis=1))
        on_right.append(np.concatenate([hi, lo, hi], axis=0))
    return np.stack(on_left), np.stack(on_right)


def split(x):
    hi = x.astype(jnp.bfloat16)
    return hi, (x - hi.astype(F32)).astype(jnp.bfloat16)


def left(table, x):
    hi, lo = split(x)
    return jnp.dot(table, jnp.concatenate([hi, hi, lo], axis=0), preferred_element_type=F32)


def right(x, table):
    hi, lo = split(x)
    return jnp.dot(jnp.concatenate([hi, hi, lo], axis=1), table, preferred_element_type=F32)


def swap_blocks(x, n):
    return jnp.concatenate(
        [
            jnp.concatenate([x[:n, :n], x[n:, :n]], axis=1),
            jnp.concatenate([x[:n, n:], x[n:, n:]], axis=1),
        ],
        axis=0,
    )


def tiling(nrow, n):
    tiles = 5 * (n // 8)
    half = -(-tiles // 2)
    return tiles, half, -(-half // nrow)


def place():
    return lax.axis_index("row"), lax.axis_index("col")


def remote(src, dst, send_sem, recv_sem, peer):
    return pltpu.make_async_remote_copy(
        src_ref=src, dst_ref=dst, send_sem=send_sem, recv_sem=recv_sem, device_id=peer, device_id_type=MESH
    )


def halo_kernel(nrow, ncol, n, obj_ref, ext_ref, send_sem, recv_sem, own_sem):
    _, height, width = obj_ref.shape
    blocks = width // n
    r, c = place()
    up, down = lax.rem(r + nrow - 1, nrow), lax.rem(r + 1, nrow)
    west, east = lax.rem(c + ncol - 1, ncol), lax.rem(c + 1, ncol)
    own = [
        pltpu.make_async_copy(obj_ref.at[:, :, b * n : (b + 1) * n], ext_ref.at[:, b, :height], own_sem.at[b])
        for b in range(blocks)
    ]
    barrier = pltpu.get_barrier_semaphore()
    for peer in ((up, c), (down, c), (r, west), (r, east)):
        pl.semaphore_signal(barrier, inc=1, device_id=peer, device_id_type=MESH)
    pl.semaphore_wait(barrier, 4)

    below = []
    for b in range(blocks):
        source = obj_ref.at[:, :n, b * n : (b + 1) * n]
        below.append(remote(source, ext_ref.at[:, b, height:], send_sem.at[b], recv_sem.at[b], (up, c)))
    right_halo = ext_ref.at[:, blocks, :height]
    corner_halo = ext_ref.at[:, blocks, height:]
    beside = remote(
        obj_ref.at[:, :, :n], right_halo, send_sem.at[blocks], recv_sem.at[blocks], (r, west)
    )
    corner = remote(
        ext_ref.at[:, 0, height:], corner_halo, send_sem.at[blocks + 1], recv_sem.at[blocks + 1], (r, west)
    )
    has_below, has_right = r < nrow - 1, c < ncol - 1

    @pl.when(r > 0)
    def _():
        below[0].start()

    @pl.when(c > 0)
    def _():
        beside.start()

    @pl.when(r > 0)
    def _():
        for one in below[1:]:
            one.start()

    for one in own:
        one.start()

    @pl.when(jnp.logical_not(has_below))
    def _():
        ext_ref[:, :, height:] = jnp.zeros((2, blocks + 1, n, n), F32)

    @pl.when(jnp.logical_not(has_right))
    def _():
        ext_ref[:, blocks, :] = jnp.zeros((2, height + n, n), F32)

    @pl.when(has_below)
    def _():
        below[0].wait_recv()

        @pl.when(c > 0)
        def _():
            corner.start()

        for one in below[1:]:
            one.wait_recv()

    for one in own:
        one.wait()

    @pl.when(has_right)
    def _():
        beside.wait_recv()

        @pl.when(has_below)
        def _():
            corner.wait_recv()

    @pl.when(r > 0)
    def _():
        for one in below:
            one.wait_send()

    @pl.when(c > 0)
    def _():
        beside.wait_send()

        @pl.when(has_below)
        def _():
            corner.wait_send()


def compute_kernel(
    shares, group, height, width,
    pos_ref, cnt_ref, ext_ref, probe_ref, meas_ref, left_ref, right_ref, grad_ref, red_ref, sums,
):
    n = probe_ref.shape[-1]
    slots = meas_ref.shape[0]
    tiles, half, share = shares
    blocks = width // n
    pr = [probe_ref[0, 0], probe_ref[0, 1]]
    pi = [probe_ref[1, 0], probe_ref[1, 1]]
    power = pr[0] * pr[0] + pi[0] * pi[0] + (pr[1] * pr[1] + pi[1] * pi[1])
    inverse = 1.0 / (jnp.max(power, keepdims=True) + 1e-06)
    lane = lax.broadcasted_iota(jnp.int32, (n, n), 1)
    grad_ref[...] = jnp.zeros(grad_ref.shape, F32)
    grad_ref[:, :blocks, :height] = ext_ref[:, :blocks, :height]
    sums[...] = jnp.zeros(sums.shape, F32)

    def some_slots(first, carry):
        pr = [probe_ref[0, 0], probe_ref[0, 1]]
        pi = [probe_ref[1, 0], probe_ref[1, 1]]
        numbers = [first * group + k for k in range(group)]
        starts, cuts, lefts = [], [], []
        for s in numbers:
            row, col = pos_ref[0, s], pos_ref[1, s]
            near = col // n
            shift = lax.rem(col, n)
            back_shift = lax.rem(n - shift, n)
            rows = pl.ds(row, n)
            starts.append((rows, near, shift))
            patch = []
            for part in range(2):
                a = pltpu.roll(ext_ref[part, near, rows], back_shift, 1)
                b = pltpu.roll(ext_ref[part, near + 1, rows], back_shift, 1)
                patch.append(jnp.where(lane < n - shift, a, b))
            cuts.append(patch)
            qr, qi = patch
            waves = jnp.concatenate(
                [
                    jnp.concatenate([pr[m] * qr - pi[m] * qi for m in range(2)], axis=1),
                    jnp.concatenate([pr[m] * qi + pi[m] * qr for m in range(2)], axis=1),
                ],
                axis=0,
            )
            lefts.append(swap_blocks(left(left_ref[1], waves), n))
        far = right(jnp.concatenate(lefts, axis=0), right_ref[0])
        scaled = []
        for k, s in enumerate(numbers):
            live = jnp.where(s < cnt_ref[0, 0], 1.0, 0.0).astype(F32)
            mine = far[2 * n * k : 2 * n * (k + 1)]
            squares = mine * mine
            intensity = squares[:n, :n] + squares[:n, n:] + (squares[n:, :n] + squares[n:, n:])
            scaling = (meas_ref[s] * lax.rsqrt(jnp.maximum(intensity, AMP_FLOOR * AMP_FLOOR)) - 1.0) * live
            scaling = jnp.concatenate([scaling, scaling], axis=1)
            scaled.append(mine * jnp.concatenate([scaling, scaling], axis=0))
        middle = right(jnp.concatenate(scaled, axis=0), right_ref[1])
        added = [0.0] * 5
        for k, s in enumerate(numbers):
            live = jnp.where(s < cnt_ref[0, 0], 1.0, 0.0).astype(F32)
            qr, qi = cuts[k]
            rows, near, shift = starts[k]
            back = left(left_ref[0], swap_blocks(middle[2 * n * k : 2 * n * (k + 1)], n))
            br = [back[:n, :n], back[:n, n:]]
            bi = [back[n:, :n], back[n:, n:]]
            for m in range(2):
                added[m] += qr * br[m] + qi * bi[m]
                added[2 + m] += qr * bi[m] - qi * br[m]
            added[4] += live * (qr * qr + qi * qi)
            terms = (
                pr[0] * br[0] + pi[0] * bi[0] + (pr[1] * br[1] + pi[1] * bi[1]),
                pr[0] * bi[0] - pi[0] * br[0] + (pr[1] * bi[1] - pi[1] * br[1]),
            )
            for part in range(2):
                term = pltpu.roll(terms[part] * inverse, shift, 1)
                grad_ref[part, near, rows] += jnp.where(lane >= shift, term, 0.0)
                grad_ref[part, near + 1, rows] += jnp.where(lane < shift, term, 0.0)
        for ch in range(5):
            sums[ch] += added[ch]
        return carry

    lax.fori_loop(0, slots // group, some_slots, 0)
    per = n // 8
    for g in range(2 * red_ref.shape[1] * share):
        h, k = divmod(g, red_ref.shape[1] * share)
        t = h * half + k
        used = k < half and t < tiles
        value = sums[t // per, 8 * (t % per) : 8 * (t % per) + 8] if used else jnp.zeros((8, n), F32)
        red_ref[h, k // share, k % share] = value


def finish_kernel(
    nrow, ncol, n, shares,
    grad_ref, red_ref, obj_ref, probe_ref,
    got0, acc0, got1, acc1, got2, every, in_right, in_corner, in_below, rim,
    send0, recv0, send1, recv1, send2, recv2, send3, recv3, send4, recv4, send_spill, recv_spill,
):
    _, height, width = obj_ref.shape
    tiles, half, share = shares
    blocks = width // n
    nchip = ncol // 2
    r, c = place()
    chip, core = c // 2, lax.rem(c, 2)
    down = lax.rem(r + 1, nrow)
    west, east = lax.rem(c + ncol - 1, ncol), lax.rem(c + 1, ncol)
    twin = (r, c + 1 - 2 * core)
    row_peer = lambda d: (lax.rem(r + d, nrow), c)
    chip_peer = lambda d: (r, lax.rem(chip + d, nchip) * 2 + core)
    barrier = pltpu.get_barrier_semaphore()
    peers = [row_peer(d) for d in range(1, nrow)] + [chip_peer(d) for d in range(1, nchip)]
    peers += [(r, west), (r, east)]
    for peer in peers:
        pl.semaphore_signal(barrier, inc=1, device_id=peer, device_id_type=MESH)
    pl.semaphore_wait(barrier, len(peers))

    pair = remote(red_ref.at[1 - core], got0, send0.at[0], recv0.at[0], twin)
    pair.start()

    corner = remote(grad_ref.at[:, blocks, height:], in_corner, send_spill.at[0], recv_spill.at[0], (r, east))
    beside = remote(grad_ref.at[:, blocks, :height], in_right, send_spill.at[1], recv_spill.at[1], (r, east))
    below = [
        remote(
            rim if b == 0 else grad_ref.at[:, b, height:],
            in_below.at[:, b], send_spill.at[2 + b], recv_spill.at[2 + b], (down, c),
        )
        for b in range(blocks)
    ]

    @pl.when(c < ncol - 1)
    def _():
        corner.start()
        beside.start()

    pair.wait_recv()
    acc0[...] = red_ref[core] + got0[...]
    first = []
    for d in range(1, nrow):
        peer = row_peer(d)
        first.append(remote(acc0.at[peer[0]], got1.at[r], send1.at[d], recv1.at[d], peer))
        first[-1].start()

    for b in range(blocks):
        obj_ref[:, :, b * n : (b + 1) * n] = grad_ref[:, b, :height]
    rim[...] = grad_ref[:, 0, height:]

    for one in first:
        one.wait_recv()
    total = acc0[r]
    for d in range(1, nrow):
        total = total + got1[lax.rem(r + nrow - d, nrow)]
    acc1[...] = total

    second = []
    for d in range(1, nchip):
        second.append(remote(acc1, got2.at[chip], send2.at[d], recv2.at[d], chip_peer(d)))
        second[-1].start()
    got2[chip] = total

    @pl.when(c > 0)
    def _():
        corner.wait_recv()
        rim[...] += in_corner[...]

    @pl.when(r < nrow - 1)
    def _():
        for one in below:
            one.start()

    for one in second:
        one.wait_recv()
    total = got2[0]
    for k in range(1, nchip):
        total = total + got2[k]
    every[core, r] = total

    third = []
    for d in range(1, nrow):
        piece = every.at[core, r]
        third.append(remote(piece, piece, send3.at[d], recv3.at[d], row_peer(d)))
        third[-1].start()

    @pl.when(c > 0)
    def _():
        beside.wait_recv()
        obj_ref[:, :, :n] += in_right[...]

    for one in third:
        one.wait_recv()
    fourth = remote(every.at[core], every.at[core], send4.at[0], recv4.at[0], twin)
    fourth.start()

    @pl.when(r > 0)
    def _():
        for b, one in enumerate(below):
            one.wait_recv()
            obj_ref[:, :n, b * n : (b + 1) * n] += in_below[:, b]

    fourth.wait_recv()

    per = n // 8

    def tile(g):
        k = g % half
        return every[g // half, k // share, k % share]

    for i in range(per):
        factor = lax.rsqrt(tile(4 * per + i) + 1.0)
        for ch in range(4):
            probe_ref[ch // 2, ch % 2, 8 * i : 8 * i + 8] = tile(ch * per + i) * factor

    for one in [pair] + first + second + third + [fourth]:
        one.wait_send()

    @pl.when(c < ncol - 1)
    def _():
        corner.wait_send()
        beside.wait_send()

    @pl.when(r < nrow - 1)
    def _():
        for one in below:
            one.wait_send()


def per_device(nrow, ncol, tables, object_field, probe_modes, measured, positions, counts):
    n = probe_modes.shape[-1]
    _, height, width = object_field.shape
    blocks, slots = width // n, measured.shape[2]
    shares = tiles, half, share = tiling(nrow, n)
    group = 4 if slots % 4 == 0 else 1
    params = functools.partial(pltpu.CompilerParams, vmem_limit_bytes=LIMIT)
    dma = pltpu.SemaphoreType.DMA
    extended = pl.pallas_call(
        functools.partial(halo_kernel, nrow, ncol, n),
        out_shape=jax.ShapeDtypeStruct((2, blocks + 1, height + n, n), F32),
        in_specs=[pl.BlockSpec(memory_space=pl.ANY)],
        out_specs=VMEM,
        scratch_shapes=[dma((blocks + 2,)), dma((blocks + 2,)), dma((blocks,))],
        compiler_params=params(collective_id=0, has_side_effects=True),
    )(object_field)
    gradient, sums = pl.pallas_call(
        functools.partial(compute_kernel, shares, group, height, width),
        out_shape=(
            jax.ShapeDtypeStruct((2, blocks + 1, height + n, n), F32),
            jax.ShapeDtypeStruct((2, nrow, share, 8, n), F32),
        ),
        in_specs=[SMEM, SMEM] + [VMEM] * 5,
        out_specs=(VMEM, VMEM),
        scratch_shapes=[pltpu.VMEM((5, n, n), F32)],
        compiler_params=params(),
    )(positions[0, 0], counts, extended, probe_modes, measured[0, 0], *tables)
    return pl.pallas_call(
        functools.partial(finish_kernel, nrow, ncol, n, shares),
        out_shape=(
            jax.ShapeDtypeStruct((2, height, width), F32),
            jax.ShapeDtypeStruct((2, 2, n, n), F32),
        ),
        in_specs=[VMEM, VMEM],
        out_specs=(VMEM, VMEM),
        scratch_shapes=[
            pltpu.VMEM((nrow, share, 8, n), F32),
            pltpu.VMEM((nrow, share, 8, n), F32),
            pltpu.VMEM((nrow, share, 8, n), F32),
            pltpu.VMEM((share, 8, n), F32),
            pltpu.VMEM((ncol // 2, share, 8, n), F32),
            pltpu.VMEM((2, nrow, share, 8, n), F32),
            pltpu.VMEM((2, height, n), F32),
            pltpu.VMEM((2, n, n), F32),
            pltpu.VMEM((2, blocks, n, n), F32),
            pltpu.VMEM((2, n, n), F32),
        ]
        + [dma((k,)) for k in (1, 1, nrow, nrow, ncol // 2, ncol // 2, nrow, nrow, 1, 1, 2 + blocks, 2 + blocks)],
        compiler_params=params(collective_id=1, has_side_effects=True),
    )(gradient, sums)


def solution(mesh):
    nrow, ncol = mesh.shape["row"], mesh.shape["col"]
    in_specs = (
        P(None, "row", "col"),
        P(),
        P("row", "col", None, None, None),
        P("row", "col", None, None),
        P("row", "col"),
    )
    out_specs = (P(None, "row", "col"), P())

    def run(object_field, probe_modes, measured, positions, counts):
        tables = [jnp.asarray(t) for t in fourier_tables(probe_modes.shape[-1])]
        return jax.shard_map(
            functools.partial(per_device, nrow, ncol, tables),
            mesh=mesh, in_specs=in_specs, out_specs=out_specs, check_vma=False,
        )(object_field, probe_modes, measured, positions, counts)

    return run
```

time: 56.8 us -> 41 us (0.72)
  Pallas kernels: 52.6 us -> 36.8 us
    pallas_call x2, Pallas kernels: 37.9 us -> 25.5 us  [the longest x1 18.7 us: per_device(): pl.pallas_call(functools.partial(finish_kernel, nrow, ncol, n, shares), o...]
    pallas_call x1, Pallas kernels: 14.6 us -> 11.2 us  [per_device(): pl.pallas_call(functools.partial(halo_kernel, nrow, ncol, n), out_shape=j...]
    unnamed x12 -> x14, local copies, waits for them, and re-layouts: 2.73 us -> 2.73 us
where the time goes in v2:
time: 41 us; the launch traced here: 40.9 us
  Pallas kernels  36.8 us (90%)
  local copies, waits for them, and re-layouts  2.73 us (7%)
  between operations  1.37 us (3%)
    pallas_call x1, Pallas kernels, per_device(): pl.pallas_call(functools.partial(finish_kernel, nrow, ncol, n, shares), o...  18.7 us
    pallas_call x1, Pallas kernels, per_device(): pl.pallas_call(functools.partial(halo_kernel, nrow, ncol, n), out_shape=j...  11.2 us
    pallas_call x1, Pallas kernels, per_device(): pl.pallas_call(functools.partial(compute_kernel, shares, group, height, w...  6.84 us
    unnamed x14, local copies, waits for them, and re-layouts  2.73 us

profile of v2, /device:TPU:0, one launch (start us, length us, event | category | flops | bytes accessed | tf_op | source)
XLA Modules:
  0.0 40.9 jit_solution(13442570909619608909)
XLA Ops:
  0.6 0.0 copy-start.5
  1.3 0.0 copy-start
  1.3 1.1 %copy-done = f32[2,384,256]{2,1,0:T(8,128)S(1)} copy-done((f32[2,384,256]{2,1,0:T(8,128)S(1)}, f32[2,384,256]{2,1,0:T(8,128)}, u32[]{:S(2)}) %copy-start) | copy-done | bytes 786456
  2.4 0.0 copy-start.1
  2.4 0.0 copy-start.2
  2.4 0.0 copy-start.3
  2.4 0.0 copy-start.4
  2.4 11.2 %shard_map.86.ext_ref = f32[2,3,512,128]{3,2,1,0:T(8,128)S(1)} custom-call(f32[2,384,256]{2,1,0:T(8,128)S(1)} %copy-done), custom_call_target="tpu_custom_call" | custom-call | tf_op jit(solution)/shard_map/pallas_call | solution.py:396
  13.7 0.0 copy-done.5
  13.7 0.0 copy-done.1
  13.7 0.0 copy-done.2
  13.7 0.0 copy-done.3
  13.7 0.0 copy-done.4
  13.7 6.8 %shard_map.87 = (f32[2,3,512,128]{3,2,1,0:T(8,128)S(1)}, f32[2,4,10,8,128]{4,3,2,1,0:T(8,128)S(1)}) custom-call(s32[2,8]{1,0:T(2,128)S(1)} %bitcast.3, s32[1,1]{1,0:T(1,128)S(6)} %copy.11.cnt_ref, f32[2,3,512,128]{3,2,1,0:T(8,128)S(1)} %shard_map.86.ext_ref, f32[2,2,128,128]{3,2,1,0:T(8,128)S(1)} %copy-done.4, f32[8,128,128]{2,1,0:T(8,128)S(1)} %bitcast.2, ...), custom_call_target="tpu_custom_call" | custom-call | tf_op jit(solution)/shard_map/pallas_call | solution.py:404
  20.6 18.7 %shard_map.88 = (f32[2,384,256]{2,1,0:T(8,128)S(1)}, f32[2,2,128,128]{3,2,1,0:T(8,128)S(1)}) custom-call(f32[2,3,512,128]{3,2,1,0:T(8,128)S(1)} %get-tuple-element.4.grad_ref, f32[2,4,10,8,128]{4,3,2,1,0:T(8,128)S(1)} %get-tuple-element.5.red_ref), custom_call_target="tpu_custom_call" | custom-call | tf_op jit(solution)/shard_map/pallas_call | solution.py:415
  39.3 0.9 %copy.12 = f32[2,384,256]{2,1,0:T(8,128)} copy(f32[2,384,256]{2,1,0:T(8,128)S(1)} %get-tuple-element.8) | data formatting | bytes 1572864
  40.2 0.7 %copy.13 = f32[2,2,128,128]{3,2,1,0:T(8,128)} copy(f32[2,2,128,128]{3,2,1,0:T(8,128)S(1)} %get-tuple-element.9) | data formatting | bytes 524288
Async XLA Ops:
  0.6 13.1 %copy-start.5 = (s32[1,1,2,8]{3,2,1,0:T(2,128)S(1)}, s32[1,1,2,8]{3,2,1,0:T(2,128)}, u32[]{:S(2)}) copy-start(s32[1,1,2,8]{3,2,1,0:T(2,128)} %param.10) | copy-start | bytes 196
  1.3 1.1 %copy-start = (f32[2,384,256]{2,1,0:T(8,128)S(1)}, f32[2,384,256]{2,1,0:T(8,128)}, u32[]{:S(2)}) copy-start(f32[2,384,256]{2,1,0:T(8,128)} %obj_ref.1) | copy-start | bytes 2359300
  2.4 11.3 %copy-start.1 = (bf16[2,768,256]{2,1,0:T(8,128)(2,1)S(1)}, bf16[2,768,256]{2,1,0:T(8,128)(2,1)}, u32[]{:S(2)}) copy-start(bf16[2,768,256]{2,1,0:T(8,128)(2,1)} %constant.5.clone.right_ref) | copy-start | bytes 2359300
  2.4 11.3 %copy-start.2 = (bf16[2,256,768]{2,1,0:T(8,128)(2,1)S(1)}, bf16[2,256,768]{2,1,0:T(8,128)(2,1)}, u32[]{:S(2)}) copy-start(bf16[2,256,768]{2,1,0:T(8,128)(2,1)} %constant.4.clone.left_ref) | copy-start | bytes 2359300
  2.4 11.3 %copy-start.3 = (f32[1,1,8,128,128]{4,3,2,1,0:T(8,128)S(1)}, f32[1,1,8,128,128]{4,3,2,1,0:T(8,128)}, u32[]{:S(2)}) copy-start(f32[1,1,8,128,128]{4,3,2,1,0:T(8,128)} %param.9) | copy-start | bytes 1572868
  2.4 11.3 %copy-start.4 = (f32[2,2,128,128]{3,2,1,0:T(8,128)S(1)}, f32[2,2,128,128]{3,2,1,0:T(8,128)}, u32[]{:S(2)}) copy-start(f32[2,2,128,128]{3,2,1,0:T(8,128)} %probe_ref.1) | copy-start | bytes 786436

commit v3 on v2

--- a/solution.py
+++ b/solution.py
@@ -15,6 +15,7 @@
 MESH = pl.DeviceIdType.MESH
 VMEM = pl.BlockSpec(memory_space=pltpu.VMEM)
 SMEM = pl.BlockSpec(memory_space=pltpu.SMEM)
+HBM = pl.BlockSpec(memory_space=pltpu.HBM)
 LIMIT = 48 * 1024 * 1024
 
 
@@ -111,21 +112,22 @@
     def _():
         beside.start()
 
+    for one in own:
+        one.start()
+
+    @pl.when(jnp.logical_not(has_below))
+    def _():
+        ext_ref[:, :, height:] = jnp.zeros((2, blocks + 1, n, n), F32)
+
+    @pl.when(jnp.logical_not(has_right))
+    def _():
+        ext_ref[:, blocks, :] = jnp.zeros((2, height + n, n), F32)
+
     @pl.when(r > 0)
     def _():
+        below[0].wait_send()
         for one in below[1:]:
             one.start()
-
-    for one in own:
-        one.start()
-
-    @pl.when(jnp.logical_not(has_below))
-    def _():
-        ext_ref[:, :, height:] = jnp.zeros((2, blocks + 1, n, n), F32)
-
-    @pl.when(jnp.logical_not(has_right))
-    def _():
-        ext_ref[:, blocks, :] = jnp.zeros((2, height + n, n), F32)
 
     @pl.when(has_below)
     def _():
@@ -151,7 +153,7 @@
 
     @pl.when(r > 0)
     def _():
-        for one in below:
+        for one in below[1:]:
             one.wait_send()
 
     @pl.when(c > 0)
@@ -254,8 +256,8 @@
 
 def finish_kernel(
     nrow, ncol, n, shares,
-    grad_ref, red_ref, obj_ref, probe_ref,
-    got0, acc0, got1, acc1, got2, every, in_right, in_corner, in_below, rim,
+    grad_ref, red_ref, obj_ref, every,
+    got0, acc0, got1, acc1, got2, in_right, in_corner, in_below, rim,
     send0, recv0, send1, recv1, send2, recv2, send3, recv3, send4, recv4, send_spill, recv_spill,
 ):
     _, height, width = obj_ref.shape
@@ -308,6 +310,12 @@
 
     for one in first:
         one.wait_recv()
+
+    @pl.when(r < nrow - 1)
+    def _():
+        for one in below[1:]:
+            one.start()
+
     total = acc0[r]
     for d in range(1, nrow):
         total = total + got1[lax.rem(r + nrow - d, nrow)]
@@ -326,8 +334,7 @@
 
     @pl.when(r < nrow - 1)
     def _():
-        for one in below:
-            one.start()
+        below[0].start()
 
     for one in second:
         one.wait_recv()
@@ -360,7 +367,26 @@
 
     fourth.wait_recv()
 
+    for one in [pair] + first + second + third + [fourth]:
+        one.wait_send()
+
+    @pl.when(c < ncol - 1)
+    def _():
+        corner.wait_send()
+        beside.wait_send()
+
+    @pl.when(r < nrow - 1)
+    def _():
+        for one in below:
+            one.wait_send()
+
+
+def result_kernel(shares, obj_ref, every, object_out, probe_out, probe, sems):
+    tiles, half, share = shares
+    n = probe.shape[-1]
     per = n // 8
+    objects = pltpu.make_async_copy(obj_ref, object_out, sems.at[0])
+    objects.start()
 
     def tile(g):
         k = g % half
@@ -369,20 +395,11 @@
     for i in range(per):
         factor = lax.rsqrt(tile(4 * per + i) + 1.0)
         for ch in range(4):
-            probe_ref[ch // 2, ch % 2, 8 * i : 8 * i + 8] = tile(ch * per + i) * factor
-
-    for one in [pair] + first + second + third + [fourth]:
-        one.wait_send()
-
-    @pl.when(c < ncol - 1)
-    def _():
-        corner.wait_send()
-        beside.wait_send()
-
-    @pl.when(r < nrow - 1)
-    def _():
-        for one in below:
-            one.wait_send()
+            probe[ch // 2, ch % 2, 8 * i : 8 * i + 8] = tile(ch * per + i) * factor
+    steps = pltpu.make_async_copy(probe, probe_out, sems.at[1])
+    steps.start()
+    objects.wait()
+    steps.wait()
 
 
 def per_device(nrow, ncol, tables, object_field, probe_modes, measured, positions, counts):
@@ -396,7 +413,7 @@
     extended = pl.pallas_call(
         functools.partial(halo_kernel, nrow, ncol, n),
         out_shape=jax.ShapeDtypeStruct((2, blocks + 1, height + n, n), F32),
-        in_specs=[pl.BlockSpec(memory_space=pl.ANY)],
+        in_specs=[HBM],
         out_specs=VMEM,
         scratch_shapes=[dma((blocks + 2,)), dma((blocks + 2,)), dma((blocks,))],
         compiler_params=params(collective_id=0, has_side_effects=True),
@@ -412,11 +429,11 @@
         scratch_shapes=[pltpu.VMEM((5, n, n), F32)],
         compiler_params=params(),
     )(positions[0, 0], counts, extended, probe_modes, measured[0, 0], *tables)
-    return pl.pallas_call(
+    object_new, total = pl.pallas_call(
         functools.partial(finish_kernel, nrow, ncol, n, shares),
         out_shape=(
             jax.ShapeDtypeStruct((2, height, width), F32),
-            jax.ShapeDtypeStruct((2, 2, n, n), F32),
+            jax.ShapeDtypeStruct((2, nrow, share, 8, n), F32),
         ),
         in_specs=[VMEM, VMEM],
         out_specs=(VMEM, VMEM),
@@ -426,7 +443,6 @@
             pltpu.VMEM((nrow, share, 8, n), F32),
             pltpu.VMEM((share, 8, n), F32),
             pltpu.VMEM((ncol // 2, share, 8, n), F32),
-            pltpu.VMEM((2, nrow, share, 8, n), F32),
             pltpu.VMEM((2, height, n), F32),
             pltpu.VMEM((2, n, n), F32),
             pltpu.VMEM((2, blocks, n, n), F32),
@@ -435,6 +451,17 @@
         + [dma((k,)) for k in (1, 1, nrow, nrow, ncol // 2, ncol // 2, nrow, nrow, 1, 1, 2 + blocks, 2 + blocks)],
         compiler_params=params(collective_id=1, has_side_effects=True),
     )(gradient, sums)
+    return pl.pallas_call(
+        functools.partial(result_kernel, shares),
+        out_shape=(
+            jax.ShapeDtypeStruct((2, height, width), F32),
+            jax.ShapeDtypeStruct((2, 2, n, n), F32),
+        ),
+        in_specs=[VMEM, VMEM],
+        out_specs=(HBM, HBM),
+        scratch_shapes=[pltpu.VMEM((2, 2, n, n), F32), dma((2,))],
+        compiler_params=params(),
+    )(object_new, total)
 
 
 def solution(mesh):

time: 41 us -> 41.6 us (1.015)
  Pallas kernels: 36.8 us -> 38.9 us
  local copies, waits for them, and re-layouts: 2.73 us -> 1.15 us
    pallas_call x1, Pallas kernels: 11.2 us -> 12.9 us  [per_device(): pl.pallas_call(functools.partial(halo_kernel, nrow, ncol, n), out_shape=j...]
    unnamed x14 -> x12, local copies, waits for them, and re-layouts: 2.73 us -> 1.15 us
    pallas_call x0 -> x1, Pallas kernels: none -> 0.98 us  [per_device(): pl.pallas_call(functools.partial(result_kernel, shares), out_shape=(jax.S...]
    pallas_call x1, Pallas kernels: 18.7 us -> 18.2 us  [per_device(): pl.pallas_call(functools.partial(finish_kernel, nrow, ncol, n, shares), o...]
where the time goes in v3:
time: 41.6 us; the launch traced here: 41.4 us
  Pallas kernels  38.9 us (94%)
  between operations  1.37 us (3%)
  local copies, waits for them, and re-layouts  1.15 us (3%)
    pallas_call x1, Pallas kernels, per_device(): pl.pallas_call(functools.partial(finish_kernel, nrow, ncol, n, shares), o...  18.2 us
    pallas_call x1, Pallas kernels, per_device(): pl.pallas_call(functools.partial(halo_kernel, nrow, ncol, n), out_shape=j...  12.9 us
    pallas_call x1, Pallas kernels, per_device(): pl.pallas_call(functools.partial(compute_kernel, shares, group, height, w...  6.87 us
    unnamed x12, local copies, waits for them, and re-layouts  1.15 us
    pallas_call x1, Pallas kernels, per_device(): pl.pallas_call(functools.partial(result_kernel, shares), out_shape=(jax.S...  0.98 us

profile of v3, /device:TPU:0, one launch (start us, length us, event | category | flops | bytes accessed | tf_op | source)
XLA Modules:
  0.0 41.4 jit_solution(4989667283360916902)
XLA Ops:
  0.6 0.0 copy-start.5
  1.3 0.0 copy-start
  1.3 1.1 %copy-done = f32[2,384,256]{2,1,0:T(8,128)S(1)} copy-done((f32[2,384,256]{2,1,0:T(8,128)S(1)}, f32[2,384,256]{2,1,0:T(8,128)}, u32[]{:S(2)}) %copy-start) | copy-done | bytes 786456
  2.4 0.0 copy-start.1
  2.4 0.0 copy-start.2
  2.4 0.0 copy-start.3
  2.4 0.0 copy-start.4
  2.4 12.9 %shard_map.86.ext_ref = f32[2,3,512,128]{3,2,1,0:T(8,128)S(1)} custom-call(f32[2,384,256]{2,1,0:T(8,128)S(1)} %copy-done), custom_call_target="tpu_custom_call" | custom-call | tf_op jit(solution)/shard_map/pallas_call | solution.py:413
  15.3 0.0 copy-done.5
  15.3 0.0 copy-done.1
  15.3 0.0 copy-done.2
  15.4 0.0 copy-done.3
  15.4 0.0 copy-done.4
  15.4 6.9 %shard_map.87 = (f32[2,3,512,128]{3,2,1,0:T(8,128)S(1)}, f32[2,4,10,8,128]{4,3,2,1,0:T(8,128)S(1)}) custom-call(s32[2,8]{1,0:T(2,128)S(1)} %bitcast.3, s32[1,1]{1,0:T(1,128)S(6)} %copy.9.cnt_ref, f32[2,3,512,128]{3,2,1,0:T(8,128)S(1)} %shard_map.86.ext_ref, f32[2,2,128,128]{3,2,1,0:T(8,128)S(1)} %copy-done.4, f32[8,128,128]{2,1,0:T(8,128)S(1)} %bitcast.2, ...), custom_call_target="tpu_custom_call" | custom-call | tf_op jit(solution)/shard_map/pallas_call | solution.py:421
  22.3 18.2 %shard_map.88 = (f32[2,384,256]{2,1,0:T(8,128)S(1)}, f32[2,4,10,8,128]{4,3,2,1,0:T(8,128)S(1)}) custom-call(f32[2,3,512,128]{3,2,1,0:T(8,128)S(1)} %get-tuple-element.6.grad_ref, f32[2,4,10,8,128]{4,3,2,1,0:T(8,128)S(1)} %get-tuple-element.7.red_ref), custom_call_target="tpu_custom_call" | custom-call | tf_op jit(solution)/shard_map/pallas_call | solution.py:432
  40.5 1.0 %shard_map.89 = (f32[2,384,256]{2,1,0:T(8,128)}, f32[2,2,128,128]{3,2,1,0:T(8,128)}) custom-call(f32[2,384,256]{2,1,0:T(8,128)S(1)} %get-tuple-element.8.obj_ref, f32[2,4,10,8,128]{4,3,2,1,0:T(8,128)S(1)} %get-tuple-element.9.every), custom_call_target="tpu_custom_call" | custom-call | tf_op jit(solution)/shard_map/pallas_call | solution.py:454
Async XLA Ops:
  0.6 14.7 %copy-start.5 = (s32[1,1,2,8]{3,2,1,0:T(2,128)S(1)}, s32[1,1,2,8]{3,2,1,0:T(2,128)}, u32[]{:S(2)}) copy-start(s32[1,1,2,8]{3,2,1,0:T(2,128)} %param.10) | copy-start | bytes 196
  1.3 1.1 %copy-start = (f32[2,384,256]{2,1,0:T(8,128)S(1)}, f32[2,384,256]{2,1,0:T(8,128)}, u32[]{:S(2)}) copy-start(f32[2,384,256]{2,1,0:T(8,128)} %obj_ref.1) | copy-start | bytes 2359300
  2.4 12.9 %copy-start.1 = (bf16[2,768,256]{2,1,0:T(8,128)(2,1)S(1)}, bf16[2,768,256]{2,1,0:T(8,128)(2,1)}, u32[]{:S(2)}) copy-start(bf16[2,768,256]{2,1,0:T(8,128)(2,1)} %constant.5.clone.right_ref) | copy-start | bytes 2359300
  2.4 12.9 %copy-start.2 = (bf16[2,256,768]{2,1,0:T(8,128)(2,1)S(1)}, bf16[2,256,768]{2,1,0:T(8,128)(2,1)}, u32[]{:S(2)}) copy-start(bf16[2,256,768]{2,1,0:T(8,128)(2,1)} %constant.4.clone.left_ref) | copy-start | bytes 2359300
  2.4 12.9 %copy-start.3 = (f32[1,1,8,128,128]{4,3,2,1,0:T(8,128)S(1)}, f32[1,1,8,128,128]{4,3,2,1,0:T(8,128)}, u32[]{:S(2)}) copy-start(f32[1,1,8,128,128]{4,3,2,1,0:T(8,128)} %param.9) | copy-start | bytes 1572868
  2.4 12.9 %copy-start.4 = (f32[2,2,128,128]{3,2,1,0:T(8,128)S(1)}, f32[2,2,128,128]{3,2,1,0:T(8,128)}, u32[]{:S(2)}) copy-start(f32[2,2,128,128]{3,2,1,0:T(8,128)} %probe_ref.1) | copy-start | bytes 786436

commit v4 on v3

--- a/solution.py
+++ b/solution.py
@@ -90,23 +90,39 @@
         pl.semaphore_signal(barrier, inc=1, device_id=peer, device_id_type=MESH)
     pl.semaphore_wait(barrier, 4)
 
-    below = []
-    for b in range(blocks):
-        source = obj_ref.at[:, :n, b * n : (b + 1) * n]
-        below.append(remote(source, ext_ref.at[:, b, height:], send_sem.at[b], recv_sem.at[b], (up, c)))
-    right_halo = ext_ref.at[:, blocks, :height]
-    corner_halo = ext_ref.at[:, blocks, height:]
-    beside = remote(
-        obj_ref.at[:, :, :n], right_halo, send_sem.at[blocks], recv_sem.at[blocks], (r, west)
-    )
-    corner = remote(
-        ext_ref.at[:, 0, height:], corner_halo, send_sem.at[blocks + 1], recv_sem.at[blocks + 1], (r, west)
-    )
+    def piece(index, src, dst, peer):
+        return remote(src, dst, send_sem.at[index], recv_sem.at[index], peer)
+
+    below = [
+        [
+            piece(
+                2 * b + part,
+                obj_ref.at[part, :n, b * n : (b + 1) * n],
+                ext_ref.at[part, b, height:],
+                (up, c),
+            )
+            for part in range(2)
+        ]
+        for b in range(blocks)
+    ]
+    later = [one for b in range(1, blocks) for one in below[b]]
+    sooner, later = later[: len(later) // 2], later[len(later) // 2 :]
+    beside = piece(2 * blocks, obj_ref.at[:, :, :n], ext_ref.at[:, blocks, :height], (r, west))
+    corner = [
+        piece(
+            2 * blocks + 1 + part,
+            ext_ref.at[part, 0, height:],
+            ext_ref.at[part, blocks, height:],
+            (r, west),
+        )
+        for part in range(2)
+    ]
     has_below, has_right = r < nrow - 1, c < ncol - 1
 
     @pl.when(r > 0)
     def _():
-        below[0].start()
+        for one in below[0]:
+            one.start()
 
     @pl.when(c > 0)
     def _():
@@ -125,19 +141,28 @@
 
     @pl.when(r > 0)
     def _():
-        below[0].wait_send()
-        for one in below[1:]:
+        for one in below[0]:
+            one.wait_send()
+        for one in sooner:
             one.start()
 
     @pl.when(has_below)
     def _():
-        below[0].wait_recv()
-
-        @pl.when(c > 0)
-        def _():
-            corner.start()
-
-        for one in below[1:]:
+        for part in range(2):
+            below[0][part].wait_recv()
+
+            @pl.when(c > 0)
+            def _():
+                corner[part].start()
+
+    @pl.when(r > 0)
+    def _():
+        for one in later:
+            one.start()
+
+    @pl.when(has_below)
+    def _():
+        for one in sooner + later:
             one.wait_recv()
 
     for one in own:
@@ -149,11 +174,12 @@
 
         @pl.when(has_below)
         def _():
-            corner.wait_recv()
+            for one in corner:
+                one.wait_recv()
 
     @pl.when(r > 0)
     def _():
-        for one in below[1:]:
+        for one in sooner + later:
             one.wait_send()
 
     @pl.when(c > 0)
@@ -162,7 +188,8 @@
 
         @pl.when(has_below)
         def _():
-            corner.wait_send()
+            for one in corner:
+                one.wait_send()
 
 
 def compute_kernel(
@@ -282,11 +309,17 @@
     pair.start()
 
     corner = remote(grad_ref.at[:, blocks, height:], in_corner, send_spill.at[0], recv_spill.at[0], (r, east))
-    beside = remote(grad_ref.at[:, blocks, :height], in_right, send_spill.at[1], recv_spill.at[1], (r, east))
+    beside = [
+        remote(
+            grad_ref.at[part, blocks, :height], in_right.at[part],
+            send_spill.at[1 + part], recv_spill.at[1 + part], (r, east),
+        )
+        for part in range(2)
+    ]
     below = [
         remote(
             rim if b == 0 else grad_ref.at[:, b, height:],
-            in_below.at[:, b], send_spill.at[2 + b], recv_spill.at[2 + b], (down, c),
+            in_below.at[:, b], send_spill.at[3 + b], recv_spill.at[3 + b], (down, c),
         )
         for b in range(blocks)
     ]
@@ -294,7 +327,7 @@
     @pl.when(c < ncol - 1)
     def _():
         corner.start()
-        beside.start()
+        beside[0].start()
 
     pair.wait_recv()
     acc0[...] = red_ref[core] + got0[...]
@@ -338,6 +371,11 @@
 
     for one in second:
         one.wait_recv()
+
+    @pl.when(c < ncol - 1)
+    def _():
+        beside[1].start()
+
     total = got2[0]
     for k in range(1, nchip):
         total = total + got2[k]
@@ -351,8 +389,8 @@
 
     @pl.when(c > 0)
     def _():
-        beside.wait_recv()
-        obj_ref[:, :, :n] += in_right[...]
+        beside[0].wait_recv()
+        obj_ref[0, :, :n] += in_right[0]
 
     for one in third:
         one.wait_recv()
@@ -365,6 +403,11 @@
             one.wait_recv()
             obj_ref[:, :n, b * n : (b + 1) * n] += in_below[:, b]
 
+    @pl.when(c > 0)
+    def _():
+        beside[1].wait_recv()
+        obj_ref[1, :, :n] += in_right[1]
+
     fourth.wait_recv()
 
     for one in [pair] + first + second + third + [fourth]:
@@ -373,7 +416,8 @@
     @pl.when(c < ncol - 1)
     def _():
         corner.wait_send()
-        beside.wait_send()
+        beside[0].wait_send()
+        beside[1].wait_send()
 
     @pl.when(r < nrow - 1)
     def _():
@@ -415,8 +459,10 @@
         out_shape=jax.ShapeDtypeStruct((2, blocks + 1, height + n, n), F32),
         in_specs=[HBM],
         out_specs=VMEM,
-        scratch_shapes=[dma((blocks + 2,)), dma((blocks + 2,)), dma((blocks,))],
-        compiler_params=params(collective_id=0, has_side_effects=True),
+        scratch_shapes=[dma((2 * blocks + 3,)), dma((2 * blocks + 3,)), dma((blocks,))],
+        compiler_params=pltpu.CompilerParams(
+            vmem_limit_bytes=60 * 1024 * 1024, collective_id=0, has_side_effects=True
+        ),
     )(object_field)
     gradient, sums = pl.pallas_call(
         functools.partial(compute_kernel, shares, group, height, width),
@@ -448,7 +494,7 @@
             pltpu.VMEM((2, blocks, n, n), F32),
             pltpu.VMEM((2, n, n), F32),
         ]
-        + [dma((k,)) for k in (1, 1, nrow, nrow, ncol // 2, ncol // 2, nrow, nrow, 1, 1, 2 + blocks, 2 + blocks)],
+        + [dma((k,)) for k in (1, 1, nrow, nrow, ncol // 2, ncol // 2, nrow, nrow, 1, 1, 3 + blocks, 3 + blocks)],
         compiler_params=params(collective_id=1, has_side_effects=True),
     )(gradient, sums)
     return pl.pallas_call(

time: 41.6 us -> 43.6 us (1.048)
  Pallas kernels: 38.9 us -> 40.5 us
    pallas_call x1, Pallas kernels: 12.9 us -> 15.4 us  [per_device(): pl.pallas_call(functools.partial(halo_kernel, nrow, ncol, n), out_shape=j...]
    pallas_call x1, Pallas kernels: 18.2 us -> 17.4 us  [per_device(): pl.pallas_call(functools.partial(finish_kernel, nrow, ncol, n, shares), o...]
where the time goes in v4:
time: 43.6 us; the launch traced here: 43.5 us
  Pallas kernels  40.5 us (93%)
  between operations  1.54 us (4%)
  local copies, waits for them, and re-layouts  1.43 us (3%)
    pallas_call x1, Pallas kernels, per_device(): pl.pallas_call(functools.partial(finish_kernel, nrow, ncol, n, shares), o...  17.4 us
    pallas_call x1, Pallas kernels, per_device(): pl.pallas_call(functools.partial(halo_kernel, nrow, ncol, n), out_shape=j...  15.4 us
    pallas_call x1, Pallas kernels, per_device(): pl.pallas_call(functools.partial(compute_kernel, shares, group, height, w...  6.64 us
    unnamed x12, local copies, waits for them, and re-layouts  1.43 us
    pallas_call x1, Pallas kernels, per_device(): pl.pallas_call(functools.partial(result_kernel, shares), out_shape=(jax.S...  0.98 us

profile of v4, /device:TPU:0, one launch (start us, length us, event | category | flops | bytes accessed | tf_op | source)
XLA Modules:
  0.0 43.5 jit_solution(16110686906362201793)
XLA Ops:
  0.6 0.0 copy-start.1
  0.6 0.0 copy-start.2
  0.7 0.0 copy-start.5
  0.7 0.0 copy-start.3
  0.7 0.0 copy-start.4
  1.5 15.4 %shard_map.86.ext_ref = f32[2,3,512,128]{3,2,1,0:T(8,128)} custom-call(f32[2,384,256]{2,1,0:T(8,128)} %obj_ref.1), custom_call_target="tpu_custom_call" | custom-call | tf_op jit(solution)/shard_map/pallas_call | solution.py:457
  16.9 0.0 copy-done.1
  16.9 0.0 copy-done.2
  17.0 0.0 copy-done.5
  17.0 0.0 copy-done.3
  17.0 0.0 copy-done.4
  17.0 0.0 copy-start
  17.0 1.4 %copy-done = f32[2,3,512,128]{3,2,1,0:T(8,128)S(1)} copy-done((f32[2,3,512,128]{3,2,1,0:T(8,128)S(1)}, f32[2,3,512,128]{3,2,1,0:T(8,128)}, u32[]{:S(2)}) %copy-start) | copy-done | bytes 1572888
  18.4 6.6 %shard_map.87 = (f32[2,3,512,128]{3,2,1,0:T(8,128)S(1)}, f32[2,4,10,8,128]{4,3,2,1,0:T(8,128)S(1)}) custom-call(s32[2,8]{1,0:T(2,128)S(1)} %bitcast.3, s32[1,1]{1,0:T(1,128)S(6)} %copy.9.cnt_ref, f32[2,3,512,128]{3,2,1,0:T(8,128)S(1)} %copy-done, f32[2,2,128,128]{3,2,1,0:T(8,128)S(1)} %copy-done.4, f32[8,128,128]{2,1,0:T(8,128)S(1)} %bitcast.2, ...), custom_call_target="tpu_custom_call" | custom-call | tf_op jit(solution)/shard_map/pallas_call | solution.py:467
  25.0 17.4 %shard_map.88 = (f32[2,384,256]{2,1,0:T(8,128)S(1)}, f32[2,4,10,8,128]{4,3,2,1,0:T(8,128)S(1)}) custom-call(f32[2,3,512,128]{3,2,1,0:T(8,128)S(1)} %get-tuple-element.6.grad_ref, f32[2,4,10,8,128]{4,3,2,1,0:T(8,128)S(1)} %get-tuple-element.7.red_ref), custom_call_target="tpu_custom_call" | custom-call | tf_op jit(solution)/shard_map/pallas_call | solution.py:478
  42.5 1.0 %shard_map.89 = (f32[2,384,256]{2,1,0:T(8,128)}, f32[2,2,128,128]{3,2,1,0:T(8,128)}) custom-call(f32[2,384,256]{2,1,0:T(8,128)S(1)} %get-tuple-element.8.obj_ref, f32[2,4,10,8,128]{4,3,2,1,0:T(8,128)S(1)} %get-tuple-element.9.every), custom_call_target="tpu_custom_call" | custom-call | tf_op jit(solution)/shard_map/pallas_call | solution.py:500
Async XLA Ops:
  0.6 16.3 %copy-start.1 = (bf16[2,768,256]{2,1,0:T(8,128)(2,1)S(1)}, bf16[2,768,256]{2,1,0:T(8,128)(2,1)}, u32[]{:S(2)}) copy-start(bf16[2,768,256]{2,1,0:T(8,128)(2,1)} %constant.5.clone.right_ref) | copy-start | bytes 2359300
  0.6 16.3 %copy-start.2 = (bf16[2,256,768]{2,1,0:T(8,128)(2,1)S(1)}, bf16[2,256,768]{2,1,0:T(8,128)(2,1)}, u32[]{:S(2)}) copy-start(bf16[2,256,768]{2,1,0:T(8,128)(2,1)} %constant.4.clone.left_ref) | copy-start | bytes 2359300
  0.7 16.3 %copy-start.5 = (s32[1,1,2,8]{3,2,1,0:T(2,128)S(1)}, s32[1,1,2,8]{3,2,1,0:T(2,128)}, u32[]{:S(2)}) copy-start(s32[1,1,2,8]{3,2,1,0:T(2,128)} %param.10) | copy-start | bytes 196
  0.7 16.3 %copy-start.3 = (f32[1,1,8,128,128]{4,3,2,1,0:T(8,128)S(1)}, f32[1,1,8,128,128]{4,3,2,1,0:T(8,128)}, u32[]{:S(2)}) copy-start(f32[1,1,8,128,128]{4,3,2,1,0:T(8,128)} %param.9) | copy-start | bytes 1572868
  0.7 16.3 %copy-start.4 = (f32[2,2,128,128]{3,2,1,0:T(8,128)S(1)}, f32[2,2,128,128]{3,2,1,0:T(8,128)}, u32[]{:S(2)}) copy-start(f32[2,2,128,128]{3,2,1,0:T(8,128)} %probe_ref.1) | copy-start | bytes 786436
  17.0 1.4 %copy-start = (f32[2,3,512,128]{3,2,1,0:T(8,128)S(1)}, f32[2,3,512,128]{3,2,1,0:T(8,128)}, u32[]{:S(2)}) copy-start(f32[2,3,512,128]{3,2,1,0:T(8,128)} %shard_map.86.ext_ref) | copy-start | bytes 4718596

commit v5 on v3

--- a/solution.py
+++ b/solution.py
@@ -257,8 +257,8 @@
 def finish_kernel(
     nrow, ncol, n, shares,
     grad_ref, red_ref, obj_ref, every,
-    got0, acc0, got1, acc1, got2, in_right, in_corner, in_below, rim,
-    send0, recv0, send1, recv1, send2, recv2, send3, recv3, send4, recv4, send_spill, recv_spill,
+    got1, acc1, got2, in_right, in_corner, in_below, rim,
+    send1, recv1, send2, recv2, send3, recv3, send_spill, recv_spill,
 ):
     _, height, width = obj_ref.shape
     tiles, half, share = shares
@@ -268,18 +268,24 @@
     chip, core = c // 2, lax.rem(c, 2)
     down = lax.rem(r + 1, nrow)
     west, east = lax.rem(c + ncol - 1, ncol), lax.rem(c + 1, ncol)
-    twin = (r, c + 1 - 2 * core)
-    row_peer = lambda d: (lax.rem(r + d, nrow), c)
+    others = [(d, other) for d in range(nrow) for other in range(2) if d or other]
+    group_peer = lambda d, other: (lax.rem(r + d, nrow), c + other * (1 - 2 * core))
     chip_peer = lambda d: (r, lax.rem(chip + d, nchip) * 2 + core)
     barrier = pltpu.get_barrier_semaphore()
-    peers = [row_peer(d) for d in range(1, nrow)] + [chip_peer(d) for d in range(1, nchip)]
+    peers = [group_peer(*o) for o in others] + [chip_peer(d) for d in range(1, nchip)]
     peers += [(r, west), (r, east)]
     for peer in peers:
         pl.semaphore_signal(barrier, inc=1, device_id=peer, device_id_type=MESH)
     pl.semaphore_wait(barrier, len(peers))
 
-    pair = remote(red_ref.at[1 - core], got0, send0.at[0], recv0.at[0], twin)
-    pair.start()
+    first = []
+    for d, other in others:
+        peer = group_peer(d, other)
+        half_of = core + other * (1 - 2 * core)
+        first.append(
+            remote(red_ref.at[half_of, peer[0]], got1.at[core, r], send1.at[other, d], recv1.at[other, d], peer)
+        )
+        first[-1].start()
 
     corner = remote(grad_ref.at[:, blocks, height:], in_corner, send_spill.at[0], recv_spill.at[0], (r, east))
     beside = remote(grad_ref.at[:, blocks, :height], in_right, send_spill.at[1], recv_spill.at[1], (r, east))
@@ -296,14 +302,6 @@
         corner.start()
         beside.start()
 
-    pair.wait_recv()
-    acc0[...] = red_ref[core] + got0[...]
-    first = []
-    for d in range(1, nrow):
-        peer = row_peer(d)
-        first.append(remote(acc0.at[peer[0]], got1.at[r], send1.at[d], recv1.at[d], peer))
-        first[-1].start()
-
     for b in range(blocks):
         obj_ref[:, :, b * n : (b + 1) * n] = grad_ref[:, b, :height]
     rim[...] = grad_ref[:, 0, height:]
@@ -316,9 +314,9 @@
         for one in below[1:]:
             one.start()
 
-    total = acc0[r]
-    for d in range(1, nrow):
-        total = total + got1[lax.rem(r + nrow - d, nrow)]
+    total = red_ref[core, r]
+    for d, other in others:
+        total = total + got1[core + other * (1 - 2 * core), lax.rem(r + nrow - d, nrow)]
     acc1[...] = total
 
     second = []
@@ -344,20 +342,15 @@
     every[core, r] = total
 
     third = []
-    for d in range(1, nrow):
+    for d, other in others:
         piece = every.at[core, r]
-        third.append(remote(piece, piece, send3.at[d], recv3.at[d], row_peer(d)))
+        third.append(remote(piece, piece, send3.at[other, d], recv3.at[other, d], group_peer(d, other)))
         third[-1].start()
 
     @pl.when(c > 0)
     def _():
         beside.wait_recv()
         obj_ref[:, :, :n] += in_right[...]
-
-    for one in third:
-        one.wait_recv()
-    fourth = remote(every.at[core], every.at[core], send4.at[0], recv4.at[0], twin)
-    fourth.start()
 
     @pl.when(r > 0)
     def _():
@@ -365,9 +358,10 @@
             one.wait_recv()
             obj_ref[:, :n, b * n : (b + 1) * n] += in_below[:, b]
 
-    fourth.wait_recv()
-
-    for one in [pair] + first + second + third + [fourth]:
+    for one in third:
+        one.wait_recv()
+
+    for one in first + second + third:
         one.wait_send()
 
     @pl.when(c < ncol - 1)
@@ -407,7 +401,7 @@
     _, height, width = object_field.shape
     blocks, slots = width // n, measured.shape[2]
     shares = tiles, half, share = tiling(nrow, n)
-    group = 4 if slots % 4 == 0 else 1
+    group = 8 if slots % 8 == 0 else 1
     params = functools.partial(pltpu.CompilerParams, vmem_limit_bytes=LIMIT)
     dma = pltpu.SemaphoreType.DMA
     extended = pl.pallas_call(
@@ -438,9 +432,7 @@
         in_specs=[VMEM, VMEM],
         out_specs=(VMEM, VMEM),
         scratch_shapes=[
-            pltpu.VMEM((nrow, share, 8, n), F32),
-            pltpu.VMEM((nrow, share, 8, n), F32),
-            pltpu.VMEM((nrow, share, 8, n), F32),
+            pltpu.VMEM((2, nrow, share, 8, n), F32),
             pltpu.VMEM((share, 8, n), F32),
             pltpu.VMEM((ncol // 2, share, 8, n), F32),
             pltpu.VMEM((2, height, n), F32),
@@ -448,7 +440,10 @@
             pltpu.VMEM((2, blocks, n, n), F32),
             pltpu.VMEM((2, n, n), F32),
         ]
-        + [dma((k,)) for k in (1, 1, nrow, nrow, ncol // 2, ncol // 2, nrow, nrow, 1, 1, 2 + blocks, 2 + blocks)],
+        + [dma(k)
+            for k in ((2, nrow), (ncol // 2,), (2, nrow), (2 + blocks,))
+            for _ in range(2)
+        ],
         compiler_params=params(collective_id=1, has_side_effects=True),
     )(gradient, sums)
     return pl.pallas_call(

time: 41.6 us -> 42.1 us (1.012)
  Pallas kernels: 38.9 us -> 39.4 us
    pallas_call x1, Pallas kernels: 18.2 us -> 18.9 us  [per_device(): pl.pallas_call(functools.partial(finish_kernel, nrow, ncol, n, shares), o...]
where the time goes in v5:
time: 42.1 us; the launch traced here: 41.9 us
  Pallas kernels  39.4 us (94%)
  between operations  1.37 us (3%)
  local copies, waits for them, and re-layouts  1.15 us (3%)
    pallas_call x1, Pallas kernels, per_device(): pl.pallas_call(functools.partial(finish_kernel, nrow, ncol, n, shares), o...  18.9 us
    pallas_call x1, Pallas kernels, per_device(): pl.pallas_call(functools.partial(halo_kernel, nrow, ncol, n), out_shape=j...  12.9 us
    pallas_call x1, Pallas kernels, per_device(): pl.pallas_call(functools.partial(compute_kernel, shares, group, height, w...  6.68 us
    unnamed x12, local copies, waits for them, and re-layouts  1.15 us
    pallas_call x1, Pallas kernels, per_device(): pl.pallas_call(functools.partial(result_kernel, shares), out_shape=(jax.S...  0.98 us

profile of v5, /device:TPU:0, one launch (start us, length us, event | category | flops | bytes accessed | tf_op | source)
XLA Modules:
  0.0 41.9 jit_solution(12984946454112221703)
XLA Ops:
  0.6 0.0 copy-start.5
  1.3 0.0 copy-start
  1.3 1.1 %copy-done = f32[2,384,256]{2,1,0:T(8,128)S(1)} copy-done((f32[2,384,256]{2,1,0:T(8,128)S(1)}, f32[2,384,256]{2,1,0:T(8,128)}, u32[]{:S(2)}) %copy-start) | copy-done | bytes 786456
  2.4 0.0 copy-start.1
  2.4 0.0 copy-start.2
  2.4 0.0 copy-start.3
  2.4 0.0 copy-start.4
  2.4 12.9 %shard_map.86.ext_ref = f32[2,3,512,128]{3,2,1,0:T(8,128)S(1)} custom-call(f32[2,384,256]{2,1,0:T(8,128)S(1)} %copy-done), custom_call_target="tpu_custom_call" | custom-call | tf_op jit(solution)/shard_map/pallas_call | solution.py:407
  15.3 0.0 copy-done.5
  15.3 0.0 copy-done.1
  15.3 0.0 copy-done.2
  15.4 0.0 copy-done.3
  15.4 0.0 copy-done.4
  15.4 6.7 %shard_map.87 = (f32[2,3,512,128]{3,2,1,0:T(8,128)S(1)}, f32[2,4,10,8,128]{4,3,2,1,0:T(8,128)S(1)}) custom-call(s32[2,8]{1,0:T(2,128)S(1)} %bitcast.3, s32[1,1]{1,0:T(1,128)S(6)} %copy.9.cnt_ref, f32[2,3,512,128]{3,2,1,0:T(8,128)S(1)} %shard_map.86.ext_ref, f32[2,2,128,128]{3,2,1,0:T(8,128)S(1)} %copy-done.4, f32[8,128,128]{2,1,0:T(8,128)S(1)} %bitcast.2, ...), custom_call_target="tpu_custom_call" | custom-call | tf_op jit(solution)/shard_map/pallas_call | solution.py:415
  22.1 18.9 %shard_map.88 = (f32[2,384,256]{2,1,0:T(8,128)S(1)}, f32[2,4,10,8,128]{4,3,2,1,0:T(8,128)S(1)}) custom-call(f32[2,3,512,128]{3,2,1,0:T(8,128)S(1)} %get-tuple-element.6.grad_ref, f32[2,4,10,8,128]{4,3,2,1,0:T(8,128)S(1)} %get-tuple-element.7.red_ref), custom_call_target="tpu_custom_call" | custom-call | tf_op jit(solution)/shard_map/pallas_call | solution.py:426
  40.9 1.0 %shard_map.89 = (f32[2,384,256]{2,1,0:T(8,128)}, f32[2,2,128,128]{3,2,1,0:T(8,128)}) custom-call(f32[2,384,256]{2,1,0:T(8,128)S(1)} %get-tuple-element.8.obj_ref, f32[2,4,10,8,128]{4,3,2,1,0:T(8,128)S(1)} %get-tuple-element.9.every), custom_call_target="tpu_custom_call" | custom-call | tf_op jit(solution)/shard_map/pallas_call | solution.py:449
Async XLA Ops:
  0.6 14.7 %copy-start.5 = (s32[1,1,2,8]{3,2,1,0:T(2,128)S(1)}, s32[1,1,2,8]{3,2,1,0:T(2,128)}, u32[]{:S(2)}) copy-start(s32[1,1,2,8]{3,2,1,0:T(2,128)} %param.10) | copy-start | bytes 196
  1.3 1.1 %copy-start = (f32[2,384,256]{2,1,0:T(8,128)S(1)}, f32[2,384,256]{2,1,0:T(8,128)}, u32[]{:S(2)}) copy-start(f32[2,384,256]{2,1,0:T(8,128)} %obj_ref.1) | copy-start | bytes 2359300
  2.4 12.9 %copy-start.1 = (bf16[2,768,256]{2,1,0:T(8,128)(2,1)S(1)}, bf16[2,768,256]{2,1,0:T(8,128)(2,1)}, u32[]{:S(2)}) copy-start(bf16[2,768,256]{2,1,0:T(8,128)(2,1)} %constant.5.clone.right_ref) | copy-start | bytes 2359300
  2.4 12.9 %copy-start.2 = (bf16[2,256,768]{2,1,0:T(8,128)(2,1)S(1)}, bf16[2,256,768]{2,1,0:T(8,128)(2,1)}, u32[]{:S(2)}) copy-start(bf16[2,256,768]{2,1,0:T(8,128)(2,1)} %constant.4.clone.left_ref) | copy-start | bytes 2359300
  2.4 12.9 %copy-start.3 = (f32[1,1,8,128,128]{4,3,2,1,0:T(8,128)S(1)}, f32[1,1,8,128,128]{4,3,2,1,0:T(8,128)}, u32[]{:S(2)}) copy-start(f32[1,1,8,128,128]{4,3,2,1,0:T(8,128)} %param.9) | copy-start | bytes 1572868
  2.4 12.9 %copy-start.4 = (f32[2,2,128,128]{3,2,1,0:T(8,128)S(1)}, f32[2,2,128,128]{3,2,1,0:T(8,128)}, u32[]{:S(2)}) copy-start(f32[2,2,128,128]{3,2,1,0:T(8,128)} %probe_ref.1) | copy-start | bytes 786436

commit v6 on v3

--- a/solution.py
+++ b/solution.py
@@ -285,16 +285,23 @@
     beside = remote(grad_ref.at[:, blocks, :height], in_right, send_spill.at[1], recv_spill.at[1], (r, east))
     below = [
         remote(
-            rim if b == 0 else grad_ref.at[:, b, height:],
-            in_below.at[:, b], send_spill.at[2 + b], recv_spill.at[2 + b], (down, c),
+            rim.at[part] if b == 0 else grad_ref.at[part, b, height:],
+            in_below.at[part, b], send_spill.at[2 + 2 * b + part], recv_spill.at[2 + 2 * b + part], (down, c),
         )
         for b in range(blocks)
+        for part in range(2)
     ]
+    early, late = below[2::2], below[3::2]
 
     @pl.when(c < ncol - 1)
     def _():
         corner.start()
         beside.start()
+
+    @pl.when(r < nrow - 1)
+    def _():
+        for one in early:
+            one.start()
 
     pair.wait_recv()
     acc0[...] = red_ref[core] + got0[...]
@@ -313,7 +320,7 @@
 
     @pl.when(r < nrow - 1)
     def _():
-        for one in below[1:]:
+        for one in late:
             one.start()
 
     total = acc0[r]
@@ -334,7 +341,8 @@
 
     @pl.when(r < nrow - 1)
     def _():
-        below[0].start()
+        for one in below[:2]:
+            one.start()
 
     for one in second:
         one.wait_recv()
@@ -361,8 +369,9 @@
 
     @pl.when(r > 0)
     def _():
-        for b, one in enumerate(below):
+        for one in below[2:] + below[:2]:
             one.wait_recv()
+        for b in range(blocks):
             obj_ref[:, :n, b * n : (b + 1) * n] += in_below[:, b]
 
     fourth.wait_recv()
@@ -407,7 +416,7 @@
     _, height, width = object_field.shape
     blocks, slots = width // n, measured.shape[2]
     shares = tiles, half, share = tiling(nrow, n)
-    group = 4 if slots % 4 == 0 else 1
+    group = 8 if slots % 8 == 0 else 1
     params = functools.partial(pltpu.CompilerParams, vmem_limit_bytes=LIMIT)
     dma = pltpu.SemaphoreType.DMA
     extended = pl.pallas_call(
@@ -448,7 +457,7 @@
             pltpu.VMEM((2, blocks, n, n), F32),
             pltpu.VMEM((2, n, n), F32),
         ]
-        + [dma((k,)) for k in (1, 1, nrow, nrow, ncol // 2, ncol // 2, nrow, nrow, 1, 1, 2 + blocks, 2 + blocks)],
+        + [dma((k,)) for k in (1, 1, nrow, nrow, ncol // 2, ncol // 2, nrow, nrow, 1, 1, 2 + 2 * blocks, 2 + 2 * blocks)],
         compiler_params=params(collective_id=1, has_side_effects=True),
     )(gradient, sums)
     return pl.pallas_call(

time: 41.6 us -> 41.5 us (level)
  no operation moved by 1% of the time
where the time goes in v6:
time: 41.5 us; the launch traced here: 41.3 us
  Pallas kernels  38.8 us (93%)
  between operations  1.37 us (3%)
  local copies, waits for them, and re-layouts  1.15 us (3%)
    pallas_call x1, Pallas kernels, per_device(): pl.pallas_call(functools.partial(finish_kernel, nrow, ncol, n, shares), o...  18.3 us
    pallas_call x1, Pallas kernels, per_device(): pl.pallas_call(functools.partial(halo_kernel, nrow, ncol, n), out_shape=j...  12.9 us
    pallas_call x1, Pallas kernels, per_device(): pl.pallas_call(functools.partial(compute_kernel, shares, group, height, w...  6.66 us
    unnamed x12, local copies, waits for them, and re-layouts  1.15 us
    pallas_call x1, Pallas kernels, per_device(): pl.pallas_call(functools.partial(result_kernel, shares), out_shape=(jax.S...  0.98 us

profile of v6, /device:TPU:0, one launch (start us, length us, event | category | flops | bytes accessed | tf_op | source)
XLA Modules:
  0.0 41.3 jit_solution(15720996975592575586)
XLA Ops:
  0.6 0.0 copy-start.5
  1.3 0.0 copy-start
  1.3 1.1 %copy-done = f32[2,384,256]{2,1,0:T(8,128)S(1)} copy-done((f32[2,384,256]{2,1,0:T(8,128)S(1)}, f32[2,384,256]{2,1,0:T(8,128)}, u32[]{:S(2)}) %copy-start) | copy-done | bytes 786456
  2.4 0.0 copy-start.1
  2.4 0.0 copy-start.2
  2.4 0.0 copy-start.3
  2.4 0.0 copy-start.4
  2.4 12.9 %shard_map.86.ext_ref = f32[2,3,512,128]{3,2,1,0:T(8,128)S(1)} custom-call(f32[2,384,256]{2,1,0:T(8,128)S(1)} %copy-done), custom_call_target="tpu_custom_call" | custom-call | tf_op jit(solution)/shard_map/pallas_call | solution.py:422
  15.3 0.0 copy-done.5
  15.3 0.0 copy-done.1
  15.3 0.0 copy-done.2
  15.4 0.0 copy-done.3
  15.4 0.0 copy-done.4
  15.4 6.7 %shard_map.87 = (f32[2,3,512,128]{3,2,1,0:T(8,128)S(1)}, f32[2,4,10,8,128]{4,3,2,1,0:T(8,128)S(1)}) custom-call(s32[2,8]{1,0:T(2,128)S(1)} %bitcast.3, s32[1,1]{1,0:T(1,128)S(6)} %copy.9.cnt_ref, f32[2,3,512,128]{3,2,1,0:T(8,128)S(1)} %shard_map.86.ext_ref, f32[2,2,128,128]{3,2,1,0:T(8,128)S(1)} %copy-done.4, f32[8,128,128]{2,1,0:T(8,128)S(1)} %bitcast.2, ...), custom_call_target="tpu_custom_call" | custom-call | tf_op jit(solution)/shard_map/pallas_call | solution.py:430
  22.0 18.3 %shard_map.88 = (f32[2,384,256]{2,1,0:T(8,128)S(1)}, f32[2,4,10,8,128]{4,3,2,1,0:T(8,128)S(1)}) custom-call(f32[2,3,512,128]{3,2,1,0:T(8,128)S(1)} %get-tuple-element.6.grad_ref, f32[2,4,10,8,128]{4,3,2,1,0:T(8,128)S(1)} %get-tuple-element.7.red_ref), custom_call_target="tpu_custom_call" | custom-call | tf_op jit(solution)/shard_map/pallas_call | solution.py:441
  40.3 1.0 %shard_map.89 = (f32[2,384,256]{2,1,0:T(8,128)}, f32[2,2,128,128]{3,2,1,0:T(8,128)}) custom-call(f32[2,384,256]{2,1,0:T(8,128)S(1)} %get-tuple-element.8.obj_ref, f32[2,4,10,8,128]{4,3,2,1,0:T(8,128)S(1)} %get-tuple-element.9.every), custom_call_target="tpu_custom_call" | custom-call | tf_op jit(solution)/shard_map/pallas_call | solution.py:463
Async XLA Ops:
  0.6 14.7 %copy-start.5 = (s32[1,1,2,8]{3,2,1,0:T(2,128)S(1)}, s32[1,1,2,8]{3,2,1,0:T(2,128)}, u32[]{:S(2)}) copy-start(s32[1,1,2,8]{3,2,1,0:T(2,128)} %param.10) | copy-start | bytes 196
  1.3 1.1 %copy-start = (f32[2,384,256]{2,1,0:T(8,128)S(1)}, f32[2,384,256]{2,1,0:T(8,128)}, u32[]{:S(2)}) copy-start(f32[2,384,256]{2,1,0:T(8,128)} %obj_ref.1) | copy-start | bytes 2359300
  2.4 12.9 %copy-start.1 = (bf16[2,768,256]{2,1,0:T(8,128)(2,1)S(1)}, bf16[2,768,256]{2,1,0:T(8,128)(2,1)}, u32[]{:S(2)}) copy-start(bf16[2,768,256]{2,1,0:T(8,128)(2,1)} %constant.5.clone.right_ref) | copy-start | bytes 2359300
  2.4 12.9 %copy-start.2 = (bf16[2,256,768]{2,1,0:T(8,128)(2,1)S(1)}, bf16[2,256,768]{2,1,0:T(8,128)(2,1)}, u32[]{:S(2)}) copy-start(bf16[2,256,768]{2,1,0:T(8,128)(2,1)} %constant.4.clone.left_ref) | copy-start | bytes 2359300
  2.4 12.9 %copy-start.3 = (f32[1,1,8,128,128]{4,3,2,1,0:T(8,128)S(1)}, f32[1,1,8,128,128]{4,3,2,1,0:T(8,128)}, u32[]{:S(2)}) copy-start(f32[1,1,8,128,128]{4,3,2,1,0:T(8,128)} %param.9) | copy-start | bytes 1572868
  2.4 12.9 %copy-start.4 = (f32[2,2,128,128]{3,2,1,0:T(8,128)S(1)}, f32[2,2,128,128]{3,2,1,0:T(8,128)}, u32[]{:S(2)}) copy-start(f32[2,2,128,128]{3,2,1,0:T(8,128)} %probe_ref.1) | copy-start | bytes 786436

commit v7 on v3

--- a/solution.py
+++ b/solution.py
@@ -86,9 +86,17 @@
         for b in range(blocks)
     ]
     barrier = pltpu.get_barrier_semaphore()
-    for peer in ((up, c), (down, c), (r, west), (r, east)):
-        pl.semaphore_signal(barrier, inc=1, device_id=peer, device_id_type=MESH)
-    pl.semaphore_wait(barrier, 4)
+    @pl.when(r < nrow - 1)
+    def _():
+        pl.semaphore_signal(barrier, inc=1, device_id=(down, c), device_id_type=MESH)
+
+    @pl.when(c < ncol - 1)
+    def _():
+        pl.semaphore_signal(barrier, inc=1, device_id=(r, east), device_id_type=MESH)
+
+    @pl.when(r + c > 0)
+    def _():
+        pl.semaphore_wait(barrier, jnp.minimum(r, 1) + jnp.minimum(c, 1))
 
     below = []
     for b in range(blocks):
@@ -273,10 +281,15 @@
     chip_peer = lambda d: (r, lax.rem(chip + d, nchip) * 2 + core)
     barrier = pltpu.get_barrier_semaphore()
     peers = [row_peer(d) for d in range(1, nrow)] + [chip_peer(d) for d in range(1, nchip)]
-    peers += [(r, west), (r, east)]
+    peers += [twin]
     for peer in peers:
         pl.semaphore_signal(barrier, inc=1, device_id=peer, device_id_type=MESH)
-    pl.semaphore_wait(barrier, len(peers))
+
+    @pl.when((core == 0) & (c > 0))
+    def _():
+        pl.semaphore_signal(barrier, inc=1, device_id=(r, west), device_id_type=MESH)
+
+    pl.semaphore_wait(barrier, len(peers) + core * jnp.minimum(ncol - 1 - c, 1))
 
     pair = remote(red_ref.at[1 - core], got0, send0.at[0], recv0.at[0], twin)
     pair.start()
@@ -311,11 +324,6 @@
     for one in first:
         one.wait_recv()
 
-    @pl.when(r < nrow - 1)
-    def _():
-        for one in below[1:]:
-            one.start()
-
     total = acc0[r]
     for d in range(1, nrow):
         total = total + got1[lax.rem(r + nrow - d, nrow)]
@@ -334,7 +342,8 @@
 
     @pl.when(r < nrow - 1)
     def _():
-        below[0].start()
+        for one in below:
+            one.start()
 
     for one in second:
         one.wait_recv()
@@ -407,7 +416,7 @@
     _, height, width = object_field.shape
     blocks, slots = width // n, measured.shape[2]
     shares = tiles, half, share = tiling(nrow, n)
-    group = 4 if slots % 4 == 0 else 1
+    group = 8 if slots % 8 == 0 else 1
     params = functools.partial(pltpu.CompilerParams, vmem_limit_bytes=LIMIT)
     dma = pltpu.SemaphoreType.DMA
     extended = pl.pallas_call(

time: 41.6 us -> 40.3 us (0.969)
  Pallas kernels: 38.9 us -> 37.4 us
    pallas_call x1, Pallas kernels: 12.9 us -> 10.4 us  [per_device(): pl.pallas_call(functools.partial(halo_kernel, nrow, ncol, n), out_shape=j...]
    pallas_call x1, Pallas kernels: 18.2 us -> 19.4 us  [per_device(): pl.pallas_call(functools.partial(finish_kernel, nrow, ncol, n, shares), o...]
where the time goes in v7:
time: 40.3 us; the launch traced here: 40 us
  Pallas kernels  37.4 us (93%)
  between operations  1.37 us (3%)
  local copies, waits for them, and re-layouts  1.15 us (3%)
    pallas_call x1, Pallas kernels, per_device(): pl.pallas_call(functools.partial(finish_kernel, nrow, ncol, n, shares), o...  19.4 us
    pallas_call x1, Pallas kernels, per_device(): pl.pallas_call(functools.partial(halo_kernel, nrow, ncol, n), out_shape=j...  10.4 us
    pallas_call x1, Pallas kernels, per_device(): pl.pallas_call(functools.partial(compute_kernel, shares, group, height, w...  6.66 us
    unnamed x12, local copies, waits for them, and re-layouts  1.15 us
    pallas_call x1, Pallas kernels, per_device(): pl.pallas_call(functools.partial(result_kernel, shares), out_shape=(jax.S...  0.98 us

profile of v7, /device:TPU:0, one launch (start us, length us, event | category | flops | bytes accessed | tf_op | source)
XLA Modules:
  0.0 40.0 jit_solution(8059855714210585102)
XLA Ops:
  0.6 0.0 copy-start.5
  1.3 0.0 copy-start
  1.3 1.1 %copy-done = f32[2,384,256]{2,1,0:T(8,128)S(1)} copy-done((f32[2,384,256]{2,1,0:T(8,128)S(1)}, f32[2,384,256]{2,1,0:T(8,128)}, u32[]{:S(2)}) %copy-start) | copy-done | bytes 786456
  2.4 0.0 copy-start.1
  2.4 0.0 copy-start.2
  2.4 0.0 copy-start.3
  2.4 0.0 copy-start.4
  2.4 10.4 %shard_map.86.ext_ref = f32[2,3,512,128]{3,2,1,0:T(8,128)S(1)} custom-call(f32[2,384,256]{2,1,0:T(8,128)S(1)} %copy-done), custom_call_target="tpu_custom_call" | custom-call | tf_op jit(solution)/shard_map/pallas_call | solution.py:422
  12.8 0.0 copy-done.5
  12.8 0.0 copy-done.1
  12.8 0.0 copy-done.2
  12.9 0.0 copy-done.3
  12.9 0.0 copy-done.4
  12.9 6.7 %shard_map.87 = (f32[2,3,512,128]{3,2,1,0:T(8,128)S(1)}, f32[2,4,10,8,128]{4,3,2,1,0:T(8,128)S(1)}) custom-call(s32[2,8]{1,0:T(2,128)S(1)} %bitcast.3, s32[1,1]{1,0:T(1,128)S(6)} %copy.9.cnt_ref, f32[2,3,512,128]{3,2,1,0:T(8,128)S(1)} %shard_map.86.ext_ref, f32[2,2,128,128]{3,2,1,0:T(8,128)S(1)} %copy-done.4, f32[8,128,128]{2,1,0:T(8,128)S(1)} %bitcast.2, ...), custom_call_target="tpu_custom_call" | custom-call | tf_op jit(solution)/shard_map/pallas_call | solution.py:430
  19.5 19.4 %shard_map.88 = (f32[2,384,256]{2,1,0:T(8,128)S(1)}, f32[2,4,10,8,128]{4,3,2,1,0:T(8,128)S(1)}) custom-call(f32[2,3,512,128]{3,2,1,0:T(8,128)S(1)} %get-tuple-element.6.grad_ref, f32[2,4,10,8,128]{4,3,2,1,0:T(8,128)S(1)} %get-tuple-element.7.red_ref), custom_call_target="tpu_custom_call" | custom-call | tf_op jit(solution)/shard_map/pallas_call | solution.py:441
  39.0 1.0 %shard_map.89 = (f32[2,384,256]{2,1,0:T(8,128)}, f32[2,2,128,128]{3,2,1,0:T(8,128)}) custom-call(f32[2,384,256]{2,1,0:T(8,128)S(1)} %get-tuple-element.8.obj_ref, f32[2,4,10,8,128]{4,3,2,1,0:T(8,128)S(1)} %get-tuple-element.9.every), custom_call_target="tpu_custom_call" | custom-call | tf_op jit(solution)/shard_map/pallas_call | solution.py:463
Async XLA Ops:
  0.6 12.2 %copy-start.5 = (s32[1,1,2,8]{3,2,1,0:T(2,128)S(1)}, s32[1,1,2,8]{3,2,1,0:T(2,128)}, u32[]{:S(2)}) copy-start(s32[1,1,2,8]{3,2,1,0:T(2,128)} %param.10) | copy-start | bytes 196
  1.3 1.1 %copy-start = (f32[2,384,256]{2,1,0:T(8,128)S(1)}, f32[2,384,256]{2,1,0:T(8,128)}, u32[]{:S(2)}) copy-start(f32[2,384,256]{2,1,0:T(8,128)} %obj_ref.1) | copy-start | bytes 2359300
  2.4 10.4 %copy-start.1 = (bf16[2,768,256]{2,1,0:T(8,128)(2,1)S(1)}, bf16[2,768,256]{2,1,0:T(8,128)(2,1)}, u32[]{:S(2)}) copy-start(bf16[2,768,256]{2,1,0:T(8,128)(2,1)} %constant.5.clone.right_ref) | copy-start | bytes 2359300
  2.4 10.4 %copy-start.2 = (bf16[2,256,768]{2,1,0:T(8,128)(2,1)S(1)}, bf16[2,256,768]{2,1,0:T(8,128)(2,1)}, u32[]{:S(2)}) copy-start(bf16[2,256,768]{2,1,0:T(8,128)(2,1)} %constant.4.clone.left_ref) | copy-start | bytes 2359300
  2.4 10.4 %copy-start.3 = (f32[1,1,8,128,128]{4,3,2,1,0:T(8,128)S(1)}, f32[1,1,8,128,128]{4,3,2,1,0:T(8,128)}, u32[]{:S(2)}) copy-start(f32[1,1,8,128,128]{4,3,2,1,0:T(8,128)} %param.9) | copy-start | bytes 1572868
  2.4 10.4 %copy-start.4 = (f32[2,2,128,128]{3,2,1,0:T(8,128)S(1)}, f32[2,2,128,128]{3,2,1,0:T(8,128)}, u32[]{:S(2)}) copy-start(f32[2,2,128,128]{3,2,1,0:T(8,128)} %probe_ref.1) | copy-start | bytes 786436
